TPU v7x, 512 devices: a whole 4x8x8 slice. The times are simulated.
512 devices in a mesh: gx: 32 (over x, z_hi, core), gy: 16 (over y, z_lo).
Axes of the slice: x: 4, y: 8, z: 8 (z_hi: 4, z_lo: 2; z = z_hi * 2 + z_lo), core: 2. Of those that a mesh axis runs over, the one named last changes fastest.
Arguments:
- velocity: float32 [3, 16, 512, 2048], P(None, None, 'gx', 'gy'), may hold values from -6 to 6
- stress: float32 [6, 16, 512, 2048], P(None, None, 'gx', 'gy'), may hold values from -6 to 6
- adj_velocity: float32 [3, 16, 512, 2048], P(None, None, 'gx', 'gy'), may hold values from -6 to 6
- adj_stress: float32 [6, 16, 512, 2048], P(None, None, 'gx', 'gy'), may hold values from -6 to 6
- lame_lambda: float32 [16, 512, 2048], P(None, 'gx', 'gy'), may hold values from 0.02 to 0.06
- shear_modulus: float32 [16, 512, 2048], P(None, 'gx', 'gy'), may hold values from 0.02 to 0.06
- buoyancy: float32 [16, 512, 2048], P(None, 'gx', 'gy'), may hold values from 0.4 to 1
- gauge_cell: int32 [32, 16, 8192], P('gx', 'gy'), may hold values from 0 to 32767
- gauge_channel: int32 [32, 16, 8192], P('gx', 'gy'), may hold values from 0 to 65535, as said below
- gauge_weight: float32 [32, 16, 8192], P('gx', 'gy'), may hold values from 0.2 to 0.8
- channel_angle: float32 [16, 65536], P('gy', 'gx'), may hold values from -3.140625 to 3.140625
- observed: float32 [16, 65536], P('gy', 'gx'), may hold values from -18 to 18
Outputs:
- velocity_next: float32 [3, 16, 512, 2048], P(None, None, 'gx', 'gy')
- stress_next: float32 [6, 16, 512, 2048], P(None, None, 'gx', 'gy')
- predicted: float32 [16, 65536], P('gy', 'gx')
- adj_velocity_next: float32 [3, 16, 512, 2048], P(None, None, 'gx', 'gy')
- adj_stress_next: float32 [6, 16, 512, 2048], P(None, None, 'gx', 'gy')
Inputs may be any that keep to these rules, and one draw needn't show every extreme that they name: `gauge_cell`: a local cell index z * 16 * 128 + x * 128 + y within the slot's own tile. `gauge_channel`: channel m of a row belongs to the tile at gx index m // 2048; a gauge slot of the tile at gx index i names a channel of tile i - 1, i or i + 1.
All inputs are finite; a program needn't handle non-finite values.
Results may differ from a plain program's by a relative error of at most 0.0003.
Values sent between devices are 32-bit elements; how exact they have to be, the bound alone decides.
No kernel may reach another device: no remote copies, remote signals or barrier semaphores. Data moves between devices by JAX's collectives and lax.ppermute only.
A program may use at most 64 MiB of HBM per device.

v0:
```python
import functools

import jax
import jax.numpy as jnp
from jax import lax
from jax.experimental import pallas as pl
from jax.experimental.pallas import tpu as pltpu
from jax.sharding import PartitionSpec as P

C1 = 9.0 / 8.0
C2 = -1.0 / 24.0
HUBER_SQUARE = 16.0
F32 = jnp.float32
BF16 = jnp.bfloat16
VMEM_LIMIT = 40 * 1024 * 1024

N_Y = 19
EDGE = 3
Y_GROUPS = 2
UNROLL = 8


def whole():
    return pl.BlockSpec(memory_space=pltpu.VMEM)


def shape(dims, dtype=F32):
    return jax.ShapeDtypeStruct(dims, dtype)


def iota(dims, axis):
    return lax.broadcasted_iota(jnp.int32, dims, axis)


def shift_y(f, e, k):
    lane = iota(f.shape, f.ndim - 1)
    n = f.shape[-1]
    if k < 0:
        return pltpu.roll(jnp.where(lane >= n + k, e, f), -k, f.ndim - 1)
    return pltpu.roll(jnp.where(lane < k, e, f), n - k, f.ndim - 1)


def shift_x(f, h, k):
    row = iota(f.shape, f.ndim - 2)
    n = f.shape[-2]
    if k < 0:
        return pltpu.roll(jnp.where(row >= n + k, h, f), -k, f.ndim - 2)
    return pltpu.roll(jnp.where(row < k, h, f), n - k, f.ndim - 2)


def ahead(shift, f, e):
    return C1 * (shift(f, e, 1) - f) + C2 * (shift(f, e, 2) - shift(f, e, -1))


def behind(shift, f, e):
    return C1 * (f - shift(f, e, -1)) + C2 * (shift(f, e, 1) - shift(f, e, -2))


def ahead_z(ref, k, z):
    return C1 * (ref[k, z + 3] - ref[k, z + 2]) + C2 * (ref[k, z + 4] - ref[k, z + 1])


def behind_z(ref, k, z):
    return C1 * (ref[k, z + 2] - ref[k, z + 1]) + C2 * (ref[k, z + 3] - ref[k, z])


def parity(axis):
    return lax.axis_index(axis) % 2


def side(par_row, first, second):
    return jnp.where(par_row == 0, first, second)


def low_half(lane):
    return lane % (2 * EDGE) < EDGE


def pack_y_kernel(par, s, v, a_s, a_v, b, out_a, out_b, s_ref, v_ref, as_ref, av_ref, b_ref, sems):
    even = par[0] == 0
    hbm = (s, v, a_s, a_v)
    vmem = (s_ref, v_ref, as_ref, av_ref)
    depth = 16 // Y_GROUPS
    copies = []
    for g in range(Y_GROUPS):
        layers = pl.ds(g * depth, depth)
        group = [
            pltpu.make_async_copy(src.at[:, layers], dst.at[:, layers], sems.at[g, i])
            for i, (src, dst) in enumerate(zip(hbm, vmem))
        ]
        group.append(pltpu.make_async_copy(b.at[layers], b_ref.at[layers], sems.at[g, 4]))
        copies.append(group)
        for copy in group:
            copy.start()

    def packed(z):
        lane = iota((16, 128), 1)
        fields = [s_ref[k, z] for k in range(6)] + [v_ref[k, z] for k in range(3)]
        fields += [as_ref[k, z] for k in range(6)] + [av_ref[k, z] for k in range(3)] + [b_ref[z]]
        out = jnp.zeros((16, 128), F32)
        for n, f in enumerate(fields):
            out = jnp.where(lane >= 2 * EDGE * n, pltpu.roll(f, 2 * EDGE * n + EDGE, 1), out)
        return out

    def body(zz, carry):
        low = low_half(iota((16, 128), 1))
        first = packed(2 * zz)
        second = packed(2 * zz + 1)
        up = jnp.where(low, first, pltpu.roll(second, EDGE, 1))
        down = jnp.where(low, pltpu.roll(first, 128 - EDGE, 1), second)
        out_a[zz] = jnp.where(even, up, down)
        out_b[zz] = jnp.where(even, down, up)
        return carry

    for g in range(Y_GROUPS):
        for copy in copies[g]:
            copy.wait()
        lax.fori_loop(g * depth // 2, (g + 1) * depth // 2, body, 0, unroll=True)


def unpack_y_all(even_y, recv_a, recv_b, fields, e_ref, main, pads, m_ref):
    zero = jnp.zeros((16, 128), F32)
    for k in range(len(fields)):
        for z in (0, 1, 18, 19):
            e_ref[k, z] = zero
    for k in range(len(pads)):
        for z in (0, 1, 18, 19):
            m_ref[k, z] = zero

    def body(zz, carry):
        low = low_half(iota((16, 128), 1))
        ra = recv_a[zz]
        rb = recv_b[zz]
        before = jnp.where(even_y, rb, ra)
        after = jnp.where(even_y, ra, rb)
        frames = (
            jnp.where(low, before, pltpu.roll(after, EDGE, 1)),
            jnp.where(low, pltpu.roll(before, 128 - EDGE, 1), after),
        )
        for sub, frame in enumerate(frames):
            z = zz * 2 + sub
            for k, n in enumerate(fields):
                e_ref[k, z + 2] = pltpu.roll(frame, (128 - EDGE - 2 * EDGE * n) % 128, 1)
            for k, n in enumerate(pads):
                m_ref[k, z + 2] = main[n, z]
        return carry

    lax.fori_loop(0, 8, body, 0, unroll=UNROLL // 2)


def pack_x_kernel(sign, fields, n_extra, par, s, v, b, recv_a, recv_b, *rest):
    extra = rest[:n_extra]
    out_a, out_b, e_ref, m_ref = rest[n_extra:]
    even_x = par[1] == 0
    unpack_y_all(par[0] == 0, recv_a, recv_b, fields, e_ref, s, (2, 4, 5), m_ref)

    def body(z, carry):
        lane = iota((16, 128), 1)
        zero = jnp.zeros((16, 128), F32)
        sxx, syy, sxy, sxz, syz = s[0, z], s[1, z], s[3, z], s[4, z], s[5, z]
        exx, eyy, exy, exz, eyz = (e_ref[k, z + 2] for k in (0, 1, 3, 4, 5))
        by = b[z]
        cx = ahead(shift_x, sxx, zero) + behind(shift_y, sxy, exy) + behind_z(m_ref, 1, z)
        cy = behind(shift_x, sxy, zero) + ahead(shift_y, syy, eyy) + behind_z(m_ref, 2, z)
        cz = behind(shift_x, sxz, zero) + behind(shift_y, syz, eyz) + ahead_z(m_ref, 0, z)
        ep = jnp.where(lane < 3, exx, zero)
        ep = jnp.where(lane >= 125, exx, ep)
        ep = jnp.where((lane >= 5) & (lane < 11), pltpu.roll(exy, 8, 1), ep)
        ep = jnp.where((lane >= 13) & (lane < 19), pltpu.roll(exz, 16, 1), ep)
        items = [v[0, z] + sign * (by * cx), v[1, z] + sign * (by * cy), v[2, z] + sign * (by * cz)]
        items += [by, sxx, sxy, sxz, ep]
        up = jnp.concatenate([f[14:16] for f in items], axis=0)
        down = jnp.concatenate([f[0:2] for f in items], axis=0)
        out_a[z] = jnp.where(even_x, up, down)
        out_b[z] = jnp.where(even_x, down, up)
        return carry

    lax.fori_loop(0, 16, body, 0, unroll=UNROLL)
    for k in range(n_extra // 2):
        out_a[16 + k] = extra[2 * k][...]
        out_b[16 + k] = extra[2 * k + 1][...]


def spread_rows(before, after, k):
    row = iota((16, 128), 0)
    left = pltpu.roll(before, (14 - 2 * k) % 16, 0) if k != 7 else before
    right = pltpu.roll(after, (16 - 2 * k) % 16, 0) if k else after
    return jnp.where(row < 8, right, left)


def step_kernel(
    sign, fields, with_rates, own_b, par, s, v, b, lam, mu, recv_ya, recv_yb, recv_xa, recv_xb, *rest
):
    if own_b:
        v_out, s_out = rest[:2]
        rest = rest[2:]
    else:
        bxa, bxb, v_out, s_out = rest[:4]
        rest = rest[4:]
    if with_rates:
        r_out = rest[0]
        rest = rest[1:]
    e_ref, m_ref, vm_ref, ve_ref, vh_ref = rest
    even_x = par[1] == 0
    unpack_y_all(par[0] == 0, recv_ya, recv_yb, fields, e_ref, s, (2, 4, 5), m_ref)
    zero = jnp.zeros((16, 128), F32)
    for k in range(3):
        for z in (0, 1, 18, 19):
            vm_ref[k, z] = zero

    def speeds(z, carry):
        xa = recv_xa[z]
        xb = recv_xb[z]
        before = jnp.where(even_x, xb, xa)
        after = jnp.where(even_x, xa, xb)
        hx, hy, hz, hb, hxx, hxy, hxz, hp = (spread_rows(before, after, k) for k in range(8))
        if not own_b:
            ba = bxa[z]
            bb = bxb[z]
            hb = spread_rows(jnp.where(even_x, bb, ba), jnp.where(even_x, ba, bb), 3)
        hpy = pltpu.roll(hp, 120, 1)
        hpz = pltpu.roll(hp, 112, 1)
        sxx, syy, sxy, sxz, syz = s[0, z], s[1, z], s[3, z], s[4, z], s[5, z]
        exx, eyy, exy, exz, eyz = (e_ref[k, z + 2] for k in (0, 1, 3, 4, 5))
        by = b[z]
        be = e_ref[9, z + 2]
        cx = ahead(shift_x, sxx, hxx) + behind(shift_y, sxy, exy) + behind_z(m_ref, 1, z)
        cy = behind(shift_x, sxy, hxy) + ahead(shift_y, syy, eyy) + behind_z(m_ref, 2, z)
        cz = behind(shift_x, sxz, hxz) + behind(shift_y, syz, eyz) + ahead_z(m_ref, 0, z)
        for k, c in enumerate((cx, cy, cz)):
            new = v[k, z] + sign * (by * c)
            vm_ref[k, z + 2] = new
            v_out[k, z] = new
        cx = ahead(shift_x, exx, hp) + behind(shift_y, exy, sxy) + behind_z(e_ref, 4, z)
        cy = behind(shift_x, exy, hpy) + ahead(shift_y, eyy, syy) + behind_z(e_ref, 5, z)
        cz = behind(shift_x, exz, hpz) + behind(shift_y, eyz, syz) + ahead_z(e_ref, 2, z)
        for k, c in enumerate((cx, cy, cz)):
            ve_ref[k, z] = e_ref[6 + k, z + 2] + sign * (be * c)
        vh_ref[0, z] = hx + sign * (hb * ahead(shift_x, zero, sxx))
        vh_ref[1, z] = hy + sign * (hb * behind(shift_x, zero, sxy))
        vh_ref[2, z] = hz + sign * (hb * behind(shift_x, zero, sxz))
        return carry

    lax.fori_loop(0, 16, speeds, 0, unroll=UNROLL)

    def rates(z, carry):
        vx, vy, vz = (vm_ref[k, z + 2] for k in range(3))
        ex, ey, ez = (ve_ref[k, z] for k in range(3))
        hx, hy, hz = (vh_ref[k, z] for k in range(3))
        r0 = behind(shift_x, vx, hx)
        r1 = behind(shift_y, vy, ey)
        r2 = behind_z(vm_ref, 2, z)
        r3 = ahead(shift_y, vx, ex) + ahead(shift_x, vy, hy)
        r4 = ahead_z(vm_ref, 0, z) + ahead(shift_x, vz, hz)
        r5 = ahead_z(vm_ref, 1, z) + ahead(shift_y, vz, ez)
        m = mu[z]
        volume = lam[z] * (r0 + r1 + r2)
        m2 = 2.0 * m
        for k, c in enumerate((volume + m2 * r0, volume + m2 * r1, volume + m2 * r2, m * r3, m * r4, m * r5)):
            s_out[k, z] = s[k, z] + sign * c
        if with_rates:
            r_out[0, z] = r0
            r_out[1, z] = r1
            r_out[2, z] = r3
        return carry

    lax.fori_loop(0, 16, rates, 0, unroll=UNROLL)


CHUNK = 4096
TILE = CHUNK // 128
ROWS = 64


def pieces(x, n):
    out = []
    for _ in range(n):
        p = x.astype(BF16)
        out.append(p)
        x = x - p.astype(F32)
    return out


def lanes_of(ref, q):
    return jnp.concatenate([ref[pl.ds(q * TILE + i, 1), :] for i in range(TILE)], axis=1)


def put_lanes(ref, k, q, row):
    for i in range(TILE):
        ref[k, pl.ds(q * TILE + i, 1), :] = row[:, 128 * i : 128 * (i + 1)]


def one_hot(index, n):
    return (iota((n, index.shape[1]), 0) == index).astype(F32).astype(BF16)


def pick(out, low, n):
    acc = jnp.zeros((8, out.shape[1]), F32)
    for t in range(n // 8):
        hit = iota(acc.shape, 0) + 8 * t == low
        acc = acc + jnp.where(hit, out[8 * t : 8 * t + 8], 0.0)
    return jnp.sum(acc, axis=0, keepdims=True)


def dot(a, b):
    return jnp.dot(a, b, preferred_element_type=F32)


def dot_nt(a, b):
    return lax.dot_general(a, b, (((1,), (1,)), ((), ())), preferred_element_type=F32)


def pick_channel(q, table, chan):
    c = lanes_of(chan, q)
    high = one_hot(c >> 7, 48)
    out = dot(table, jnp.concatenate([high] * 3, axis=0))
    return pick(out, c & 127, 128)


def channel_table(rows):
    return jnp.concatenate(pieces(rows.T, 3), axis=1)


def sample_kernel(par, cell, chan_raw, weight, angle_a, angle, angle_b, rates, part, trig, chan, table, rows, vals):
    chan[...] = chan_raw[...] - par[2]
    even_x = par[1] == 0
    aa = angle_a[...]
    ab = angle_b[...]
    angles = jnp.concatenate([jnp.where(even_x, ab, aa), angle[...], jnp.where(even_x, aa, ab)], axis=0)
    ang = channel_table(angles)
    for k in range(3):
        hi, lo = pieces(rates[k].T, 2)
        table[128 * k : 128 * (k + 1)] = hi
        table[384 + 128 * k : 384 + 128 * (k + 1)] = lo

    def gather(q, carry):
        put_lanes(rows, 0, q, pick_channel(q, ang, chan))
        c = lanes_of(cell, q)
        out = dot(table[...], one_hot(c >> 7, 256))
        low = c & 127
        for k in range(3):
            both = out[128 * k : 128 * (k + 1)] + out[384 + 128 * k : 384 + 128 * (k + 1)]
            put_lanes(rows, 1 + k, q, pick(both, low, 128))
        return carry

    lax.fori_loop(0, 8192 // CHUNK, gather, 0)
    theta = rows[0]
    cosine = jnp.cos(theta)
    sine = jnp.sin(theta)
    w = weight[...]
    t0 = w * (cosine * cosine)
    t1 = w * (sine * sine)
    t2 = w * (cosine * sine)
    trig[0] = t0
    trig[1] = t1
    trig[2] = t2
    value = t0 * rows[1] + t1 * rows[2] + t2 * rows[3]
    for k, p in enumerate(pieces(value, 3)):
        vals[k] = p.astype(F32)

    def scatter(q, acc):
        c = lanes_of(chan, q)
        hit = iota((48, CHUNK), 0) == c >> 7
        a = jnp.concatenate([jnp.where(hit, lanes_of(vals.at[k], q), 0.0) for k in range(3)], axis=0)
        return acc + dot_nt(a.astype(BF16), one_hot(c & 127, 128))

    acc = lax.fori_loop(0, 8192 // CHUNK, scatter, jnp.zeros((144, 128), F32))
    part[...] = acc[0:48] + acc[48:96] + acc[96:144]


def deposit_kernel(par, cell, chan_raw, trig, robust_a, robust, robust_b, pulled, out, chan, vals, acc):
    chan[...] = chan_raw[...] - par[2]
    even_x = par[1] == 0
    ra = robust_a[...]
    rb = robust_b[...]
    tab = channel_table(
        jnp.concatenate([jnp.where(even_x, rb, ra), robust[...], jnp.where(even_x, ra, rb)], axis=0)
    )

    def gather(q, carry):
        put_lanes(vals, 6, q, pick_channel(q, tab, chan))
        return carry

    lax.fori_loop(0, 8192 // CHUNK, gather, 0)
    rob = vals[6]
    for k in range(3):
        for i, p in enumerate(pieces(trig[k] * rob, 2)):
            vals[2 * k + i] = p.astype(F32)
    acc[...] = jnp.zeros(acc.shape, F32)

    def place(q, carry):
        c = lanes_of(cell, q)
        hit = iota((128, CHUNK), 0) == c & 127
        b = jnp.concatenate([jnp.where(hit, lanes_of(vals.at[k], q), 0.0).astype(BF16) for k in range(6)], axis=0)
        acc[...] += dot_nt(one_hot(c >> 7, 256), b)
        return carry

    lax.fori_loop(0, 8192 // CHUNK, place, 0)
    for k in (2, 4, 5):
        out[k] = pulled[k]
    for n, k in enumerate((0, 1, 3)):
        out[k] = pulled[k] + acc[:, 256 * n : 256 * n + 128] + acc[:, 256 * n + 128 : 256 * n + 256]


def pairs(axis, first):
    size = lax.axis_size(axis)
    route = []
    for i in range(first, size - 1, 2):
        route += [(i, i + 1), (i + 1, i)]
    return route


def swap(a, b, axis):
    return (lax.ppermute(a, axis, pairs(axis, 0)), lax.ppermute(b, axis, pairs(axis, 1)))


def call(kernel, outs, n_in, scratch, name, space=pltpu.VMEM):
    return pl.pallas_call(
        kernel,
        out_shape=outs,
        in_specs=[pl.BlockSpec(memory_space=pltpu.SMEM)] + [pl.BlockSpec(memory_space=space)] * n_in,
        out_specs=jax.tree.map(lambda _: whole(), outs),
        scratch_shapes=scratch,
        compiler_params=pltpu.CompilerParams(vmem_limit_bytes=VMEM_LIMIT),
        name=name,
    )


def shards(
    velocity,
    stress,
    adj_velocity,
    adj_stress,
    lame_lambda,
    shear_modulus,
    buoyancy,
    gauge_cell,
    gauge_channel,
    gauge_weight,
    channel_angle,
    observed,
):
    owned = observed.shape[1]
    gx = lax.axis_index("gx")
    gy = lax.axis_index("gy")
    par = jnp.stack([gy % 2, gx % 2, (gx - 1) * owned]).astype(jnp.int32)
    even_x = gx % 2 == 0
    slots = (ROWS, 128)
    cell = gauge_cell.reshape(slots)
    chan = gauge_channel.reshape(slots)
    weight = gauge_weight.reshape(slots)
    angle = channel_angle.reshape(16, 128)

    slab = shape((8, 16, 128))
    msg_a, msg_b = call(
        pack_y_kernel,
        (slab, slab),
        5,
        [pltpu.VMEM(f.shape, F32) for f in (stress, velocity, adj_stress, adj_velocity, buoyancy)]
        + [pltpu.SemaphoreType.DMA((Y_GROUPS, 5))],
        "pack_y",
        pltpu.HBM,
    )(
        par, stress, velocity, adj_stress, adj_velocity, buoyancy
    )
    ya, yb = swap(msg_a, msg_b, "gy")

    e_scratch = pltpu.VMEM((10, 20, 16, 128), F32)
    m_scratch = pltpu.VMEM((3, 20, 16, 128), F32)
    fields_f = tuple(range(9)) + (18,)
    fields_a = tuple(range(9, 18)) + (18,)
    msg = shape((17, 16, 128))
    fa, fb = call(
        functools.partial(pack_x_kernel, 1.0, fields_f, 2), (msg, msg), 7, [e_scratch, m_scratch], "pack_x"
    )(par, stress, velocity, buoyancy, ya, yb, angle, angle)
    fa, fb = swap(fa, fb, "gx")
    msg = shape((16, 16, 128))
    aa, ab = call(
        functools.partial(pack_x_kernel, -1.0, fields_a, 0), (msg, msg), 5, [e_scratch, m_scratch], "pack_x_adj"
    )(par, adj_stress, adj_velocity, buoyancy, ya, yb)

    speed = shape((3, 16, 16, 128))
    tensor = shape((6, 16, 16, 128))
    v_scratch = [pltpu.VMEM((3, 20, 16, 128), F32)] + [pltpu.VMEM((3, 16, 16, 128), F32)] * 2
    velocity_next, stress_next, rates = call(
        functools.partial(step_kernel, 1.0, fields_f, True, True),
        (speed, tensor, speed),
        9,
        [e_scratch, m_scratch] + v_scratch,
        "step",
    )(par, stress, velocity, buoyancy, lame_lambda, shear_modulus, ya, yb, fa, fb)

    part, trig = call(
        sample_kernel,
        (shape((48, 128)), shape((3,) + slots)),
        7,
        [
            pltpu.VMEM(slots, jnp.int32),
            pltpu.VMEM((768, 256), BF16),
            pltpu.VMEM((4,) + slots, F32),
            pltpu.VMEM((3,) + slots, F32),
        ],
        "sample",
    )(par, cell, chan, weight, fa[16], angle, fb[16], rates.reshape(3, 256, 128))

    to_after = part[32:48]
    to_before = part[0:16]
    send_a = jnp.concatenate([aa, jnp.where(even_x, to_after, to_before)[None]], axis=0)
    send_b = jnp.concatenate([ab, jnp.where(even_x, to_before, to_after)[None]], axis=0)
    aa, ab = swap(send_a, send_b, "gx")
    predicted = part[16:32] + aa[16] + ab[16]
    misfit = predicted - observed.reshape(16, 128)
    robust = misfit / jnp.sqrt(HUBER_SQUARE + misfit * misfit)
    robust_a, robust_b = swap(robust, robust, "gx")

    adj_velocity_next, pulled = call(
        functools.partial(step_kernel, -1.0, fields_a, False, False),
        (speed, tensor),
        11,
        [e_scratch, m_scratch] + v_scratch,
        "step_adj",
    )(par, adj_stress, adj_velocity, buoyancy, lame_lambda, shear_modulus, ya, yb, aa, ab, fa, fb)

    adj_stress_next = call(
        deposit_kernel,
        shape((6, 256, 128)),
        7,
        [
            pltpu.VMEM(slots, jnp.int32),
            pltpu.VMEM((7,) + slots, F32),
            pltpu.VMEM((256, 768), F32),
        ],
        "deposit",
    )(par, cell, chan, trig, robust_a, robust, robust_b, pulled.reshape(6, 256, 128)).reshape(tensor.shape)
    return (velocity_next, stress_next, predicted.reshape(1, owned), adj_velocity_next, adj_stress_next)


def solution(mesh):
    field = P(None, None, "gx", "gy")
    scalar = P(None, "gx", "gy")
    slot = P("gx", "gy", None)
    row = P("gy", "gx")
    return jax.shard_map(
        shards,
        mesh=mesh,
        in_specs=(field,) * 4 + (scalar,) * 3 + (slot,) * 3 + (row,) * 2,
        out_specs=(field, field, row, field, field),
        check_vma=False,
    )
```

profile of v0, /device:TPU:31, one launch (start us, length us, event | category | flops | bytes accessed | tf_op | source)
XLA Modules:
  0.0 80.4 jit_solution(3254324227562851387)
XLA Ops:
  0.6 0.1 pad_add_fusion.par
  0.7 1.1 %copy-done = f32[6,16,16,128]{3,2,1,0:T(8,128)S(1)} copy-done((f32[6,16,16,128]{3,2,1,0:T(8,128)S(1)}, f32[6,16,16,128]{3,2,1,0:T(8,128)}, u32[]{:S(2)}) %copy-start) | copy-done | bytes 786456
  1.9 1.1 %copy-done.2 = f32[6,16,16,128]{3,2,1,0:T(8,128)S(1)} copy-done((f32[6,16,16,128]{3,2,1,0:T(8,128)S(1)}, f32[6,16,16,128]{3,2,1,0:T(8,128)}, u32[]{:S(2)}) %copy-start.2) | copy-done | bytes 786456
  3.0 1.0 %copy-done.4 = f32[3,16,16,128]{3,2,1,0:T(8,128)S(1)} copy-done((f32[3,16,16,128]{3,2,1,0:T(8,128)S(1)}, f32[3,16,16,128]{3,2,1,0:T(8,128)}, u32[]{:S(2)}) %copy-start.4) | copy-done | bytes 393240
  4.0 1.0 %copy-done.6 = f32[3,16,16,128]{3,2,1,0:T(8,128)S(1)} copy-done((f32[3,16,16,128]{3,2,1,0:T(8,128)S(1)}, f32[3,16,16,128]{3,2,1,0:T(8,128)}, u32[]{:S(2)}) %copy-start.6) | copy-done | bytes 393240
  5.0 0.9 %copy-done.8 = f32[16,16,128]{2,1,0:T(8,128)S(1)} copy-done((f32[16,16,128]{2,1,0:T(8,128)S(1)}, f32[16,16,128]{2,1,0:T(8,128)}, u32[]{:S(2)}) %copy-start.8) | copy-done | bytes 131096
  5.9 2.7 %pack_y.1 = (f32[8,16,128]{2,1,0:T(8,128)S(1)}, f32[8,16,128]{2,1,0:T(8,128)S(1)}) custom-call(s32[3]{0:T(128)S(1)} %pad_add_fusion.par, f32[6,16,16,128]{3,2,1,0:T(8,128)S(1)} %copy-done.2, f32[3,16,16,128]{3,2,1,0:T(8,128)S(1)} %copy-done.6, f32[6,16,16,128]{3,2,1,0:T(8,128)S(1)} %copy-done, f32[3,16,16,128]{3,2,1,0:T(8,128)S(1)} %copy-done.4, ...), custom_call_target="tpu_custom_call" | custom-call | tf_op jit(solution)/shard_map/pack_y/pallas_call | solution.py:455
  8.6 0.0 copy-start.1
  8.6 4.1 %collective-permute-start = (f32[8,16,128]{2,1,0:T(8,128)S(1)}, f32[8,16,128]{2,1,0:T(8,128)S(1)}, u32[]{:S(2)}, u32[]{:S(2)}) collective-permute-start(f32[8,16,128]{2,1,0:T(8,128)S(1)} %get-tuple-element.18), channel_id=1, source_target_pairs={{0,1},{1,0},{2,3},{3,2},{4,5},{5,4},{6,7},{7,6},{8,9},{9,8},{10,11... | collective-permute-start | bytes 196616 | tf_op jit(solution)/shard_map/ppermute | solution.py:414
  12.7 1.9 %collective-permute-start.1 = (f32[8,16,128]{2,1,0:T(8,128)S(1)}, f32[8,16,128]{2,1,0:T(8,128)S(1)}, u32[]{:S(2)}, u32[]{:S(2)}) collective-permute-start(f32[8,16,128]{2,1,0:T(8,128)S(1)} %get-tuple-element.19), channel_id=1, source_target_pairs={{1,2},{2,1},{3,4},{4,3},{5,6},{6,5},{7,8},{8,7},{9,10},{10,9},{11,... | collective-permute-start | bytes 196616 | tf_op jit(solution)/shard_map/ppermute | solution.py:414
  14.6 0.0 collective-permute-done.recv_a.recv_ya
  14.6 4.0 %collective-permute-done.1.recv_b.recv_yb = f32[8,16,128]{2,1,0:T(8,128)S(1)} collective-permute-done((f32[8,16,128]{2,1,0:T(8,128)S(1)}, f32[8,16,128]{2,1,0:T(8,128)S(1)}, u32[]{:S(2)}, u32[]{:S(2)}) %collective-permute-start.1) | collective-permute-done | bytes 65568 | tf_op jit(solution)/shard_map/ppermute | solution.py:414
  18.6 0.0 copy-done.14
  18.6 2.0 %pack_x.1 = (f32[17,16,128]{2,1,0:T(8,128)S(1)}, f32[17,16,128]{2,1,0:T(8,128)S(1)}) custom-call(s32[3]{0:T(128)S(1)} %pad_add_fusion.par, f32[6,16,16,128]{3,2,1,0:T(8,128)S(1)} %copy-done.2, f32[3,16,16,128]{3,2,1,0:T(8,128)S(1)} %copy-done.6, f32[16,16,128]{2,1,0:T(8,128)S(1)} %copy-done.8, f32[8,16,128]{2,1,0:T(8,128)S(1)} %collective-permute-done.recv_a.recv_ya, ...), custom_call_target="tpu_custom_call" | custom-call | tf_op jit(solution)/shard_map/pack_x/pallas_call | solution.py:473
  20.6 0.0 copy-start.3
  20.6 4.1 %collective-permute-start.2 = (f32[17,16,128]{2,1,0:T(8,128)S(1)}, f32[17,16,128]{2,1,0:T(8,128)S(1)}, u32[]{:S(2)}, u32[]{:S(2)}) collective-permute-start(f32[17,16,128]{2,1,0:T(8,128)S(1)} %get-tuple-element.20), channel_id=1, source_target_pairs={{0,16},{16,0},{32,48},{48,32},{64,80},{80,64},{96,112},{112,96},{1... | collective-permute-start | bytes 417800 | tf_op jit(solution)/shard_map/ppermute | solution.py:414
  24.8 0.0 copy-start.7
  24.8 0.0 copy-start.10
  24.8 0.0 copy-start.11
  24.8 5.8 %collective-permute-start.3 = (f32[17,16,128]{2,1,0:T(8,128)S(1)}, f32[17,16,128]{2,1,0:T(8,128)S(1)}, u32[]{:S(2)}, u32[]{:S(2)}) collective-permute-start(f32[17,16,128]{2,1,0:T(8,128)S(1)} %get-tuple-element.21), channel_id=1, source_target_pairs={{16,32},{32,16},{48,64},{64,48},{80,96},{96,80},{112,128},{128,112... | collective-permute-start | bytes 417800 | tf_op jit(solution)/shard_map/ppermute | solution.py:414
  30.7 0.0 copy-done.1
  30.7 0.0 copy-done.5
  30.7 0.0 copy-done.9
  30.7 1.9 %pack_x_adj.1 = (f32[16,16,128]{2,1,0:T(8,128)S(1)}, f32[16,16,128]{2,1,0:T(8,128)S(1)}) custom-call(s32[3]{0:T(128)S(1)} %pad_add_fusion.par, f32[6,16,16,128]{3,2,1,0:T(8,128)S(1)} %copy-done.1, f32[3,16,16,128]{3,2,1,0:T(8,128)S(1)} %copy-done.5, f32[16,16,128]{2,1,0:T(8,128)S(1)} %copy-done.9, f32[8,16,128]{2,1,0:T(8,128)S(1)} %collective-permute-done.recv_a.recv_ya, ...), custom_call_target="tpu_custom_call" | custom-call | tf_op jit(solution)/shard_map/pack_x_adj/pallas_call | solution.py:478
  32.6 0.0 collective-permute-done.2.recv_xa.rest_0_
  32.7 2.2 %collective-permute-done.3.recv_xb.rest_1_ = f32[17,16,128]{2,1,0:T(8,128)S(1)} collective-permute-done((f32[17,16,128]{2,1,0:T(8,128)S(1)}, f32[17,16,128]{2,1,0:T(8,128)S(1)}, u32[]{:S(2)}, u32[]{:S(2)}) %collective-permute-start.3) | collective-permute-done | bytes 139296 | tf_op jit(solution)/shard_map/ppermute | solution.py:414
  34.9 0.0 copy-done.3
  34.9 0.0 copy-done.7
  34.9 0.0 copy-done.10
  34.9 0.0 copy-start.12
  34.9 0.0 copy-start.13
  34.9 0.0 copy-start.15
  34.9 3.8 %step.1 = (f32[3,16,16,128]{3,2,1,0:T(8,128)}, f32[6,16,16,128]{3,2,1,0:T(8,128)}, f32[3,16,16,128]{3,2,1,0:T(8,128)S(1)}) custom-call(s32[3]{0:T(128)S(1)} %pad_add_fusion.par, f32[6,16,16,128]{3,2,1,0:T(8,128)S(1)} %copy-done.3, f32[3,16,16,128]{3,2,1,0:T(8,128)S(1)} %copy-done.7, f32[16,16,128]{2,1,0:T(8,128)S(1)} %copy-done.9, ...), custom_call_target="tpu_custom_call" | custom-call | tf_op jit(solution)/shard_map/step/pallas_call | solution.py:485
  38.8 0.0 copy-done.12
  38.8 0.0 copy-done.15
  38.8 6.9 %sample.1 = (f32[48,128]{1,0:T(8,128)S(1)}, f32[3,64,128]{2,1,0:T(8,128)S(1)}) custom-call(s32[3]{0:T(128)S(1)} %pad_add_fusion.par, s32[64,128]{1,0:T(8,128)S(1)} %bitcast.34, s32[64,128]{1,0:T(8,128)S(1)} %bitcast.36, f32[64,128]{1,0:T(8,128)S(1)} %bitcast.41, f32[16,128]{1,0:T(8,128)S(1)} %slice_bitcast_fusion.3.angle_a, f32[16,128]{1,0:T(8,128)S(1)} %bitcast.40, ...), custom_call_target="tpu_custom_call" | custom-call | tf_op jit(solution)/shard_map/sample/pallas_call | solution.py:493
  45.7 3.1 %collective-permute-start.5 = (f32[17,16,128]{2,1,0:T(8,128)S(1)}, f32[17,16,128]{2,1,0:T(8,128)S(1)}, u32[]{:S(2)}, u32[]{:S(2)}) collective-permute-start(f32[17,16,128]{2,1,0:T(8,128)S(1)} %pad_maximum_fusion.1), channel_id=1, source_target_pairs={{16,32},{32,16},{48,64},{64,48},{80,96},{96,80},{112,128},{128,112... | collective-permute-start | bytes 417800 | tf_op jit(solution)/shard_map/ppermute | solution.py:414
  48.9 0.0 copy-start.16
  48.9 10.1 %collective-permute-start.4 = (f32[17,16,128]{2,1,0:T(8,128)S(1)}, f32[17,16,128]{2,1,0:T(8,128)S(1)}, u32[]{:S(2)}, u32[]{:S(2)}) collective-permute-start(f32[17,16,128]{2,1,0:T(8,128)S(1)} %pad_maximum_fusion), channel_id=1, source_target_pairs={{0,16},{16,0},{32,48},{48,32},{64,80},{80,64},{96,112},{112,96},{1... | collective-permute-start | bytes 417800 | tf_op jit(solution)/shard_map/ppermute | solution.py:414
  59.1 0.0 collective-permute-done.5.recv_xb
  59.1 1.0 %collective-permute-done.4.recv_xa = f32[17,16,128]{2,1,0:T(8,128)S(1)} collective-permute-done((f32[17,16,128]{2,1,0:T(8,128)S(1)}, f32[17,16,128]{2,1,0:T(8,128)S(1)}, u32[]{:S(2)}, u32[]{:S(2)}) %collective-permute-start.4) | collective-permute-done | bytes 139296 | tf_op jit(solution)/shard_map/ppermute | solution.py:414
  60.0 0.6 rsqrt_multiply_fusion
  60.6 1.9 %collective-permute-start.7 = (f32[16,128]{1,0:T(8,128)S(1)}, f32[16,128]{1,0:T(8,128)S(1)}, u32[]{:S(2)}, u32[]{:S(2)}) collective-permute-start(f32[16,128]{1,0:T(8,128)S(1)} %get-tuple-element.31.robust), channel_id=1, source_target_pairs={{16,32},{32,16},{48,64},{64,48},{80,96},{96,80},{112,128},{128,112... | collective-permute-start | bytes 24584 | tf_op jit(solution)/shard_map/ppermute | solution.py:414
  62.6 7.7 %collective-permute-start.6 = (f32[16,128]{1,0:T(8,128)S(1)}, f32[16,128]{1,0:T(8,128)S(1)}, u32[]{:S(2)}, u32[]{:S(2)}) collective-permute-start(f32[16,128]{1,0:T(8,128)S(1)} %get-tuple-element.31.robust), channel_id=1, source_target_pairs={{0,16},{16,0},{32,48},{48,32},{64,80},{80,64},{96,112},{112,96},{1... | collective-permute-start | bytes 24584 | tf_op jit(solution)/shard_map/ppermute | solution.py:414
  70.3 3.5 %step_adj.1 = (f32[3,16,16,128]{3,2,1,0:T(8,128)}, f32[6,16,16,128]{3,2,1,0:T(8,128)S(1)}) custom-call(s32[3]{0:T(128)S(1)} %pad_add_fusion.par, f32[6,16,16,128]{3,2,1,0:T(8,128)S(1)} %copy-done.1, f32[3,16,16,128]{3,2,1,0:T(8,128)S(1)} %copy-done.5, f32[16,16,128]{2,1,0:T(8,128)S(1)} %copy-done.9, f32[16,16,128]{2,1,0:T(8,128)S(1)} %copy-done.10, ...), custom_call_target="tpu_custom_call" | custom-call | tf_op jit(solution)/shard_map/step_adj/pallas_call | solution.py:516
  73.8 0.0 collective-permute-done.7.robust_b
  73.8 0.0 collective-permute-done.6.robust_a
  73.8 6.6 %deposit.1 = f32[6,256,128]{2,1,0:T(8,128)} custom-call(s32[3]{0:T(128)S(1)} %pad_add_fusion.par, s32[64,128]{1,0:T(8,128)S(1)} %bitcast.35, s32[64,128]{1,0:T(8,128)S(1)} %bitcast.37, f32[3,64,128]{2,1,0:T(8,128)S(1)} %get-tuple-element.29.trig, f32[16,128]{1,0:T(8,128)S(1)} %collective-permute-done.6.robust_a, f32[16,128]{1,0:T(8,128)S(1)} %get-tuple-element.31.robust, ...), custom_call_target="tpu_custom_call" | custom-call | tf_op jit(solution)/shard_map/deposit/pallas_call | solution.py:524
  (16 shorter events, 0.1 us)
Async XLA Ops:
  0.7 1.1 %copy-start = (f32[6,16,16,128]{3,2,1,0:T(8,128)S(1)}, f32[6,16,16,128]{3,2,1,0:T(8,128)}, u32[]{:S(2)}) copy-start(f32[6,16,16,128]{3,2,1,0:T(8,128)} %s.9) | copy-start | bytes 2359300
  1.9 1.1 %copy-start.2 = (f32[6,16,16,128]{3,2,1,0:T(8,128)S(1)}, f32[6,16,16,128]{3,2,1,0:T(8,128)}, u32[]{:S(2)}) copy-start(f32[6,16,16,128]{3,2,1,0:T(8,128)} %s.7) | copy-start | bytes 2359300
  3.0 1.0 %copy-start.4 = (f32[3,16,16,128]{3,2,1,0:T(8,128)S(1)}, f32[3,16,16,128]{3,2,1,0:T(8,128)}, u32[]{:S(2)}) copy-start(f32[3,16,16,128]{3,2,1,0:T(8,128)} %v.9) | copy-start | bytes 1179652
  4.0 1.0 %copy-start.6 = (f32[3,16,16,128]{3,2,1,0:T(8,128)S(1)}, f32[3,16,16,128]{3,2,1,0:T(8,128)}, u32[]{:S(2)}) copy-start(f32[3,16,16,128]{3,2,1,0:T(8,128)} %v.7) | copy-start | bytes 1179652
  5.0 0.9 %copy-start.8 = (f32[16,16,128]{2,1,0:T(8,128)S(1)}, f32[16,16,128]{2,1,0:T(8,128)}, u32[]{:S(2)}) copy-start(f32[16,16,128]{2,1,0:T(8,128)} %b.9) | copy-start | bytes 393220
  5.9 12.7 %copy-start.14 = (f32[1,2048]{1,0:T(1,128)S(1)}, f32[1,2048]{1,0:T(1,128)}, u32[]{:S(2)}) copy-start(f32[1,2048]{1,0:T(1,128)} %param.22) | copy-start | bytes 24580
  8.6 22.1 %copy-start.1 = (f32[6,16,16,128]{3,2,1,0:T(8,128)S(1)}, f32[6,16,16,128]{3,2,1,0:T(8,128)}, u32[]{:S(2)}) copy-start(f32[6,16,16,128]{3,2,1,0:T(8,128)} %s.9) | copy-start | bytes 2359300
  8.6 6.1 %collective-permute-start = (f32[8,16,128]{2,1,0:T(8,128)S(1)}, f32[8,16,128]{2,1,0:T(8,128)S(1)}, u32[]{:S(2)}, u32[]{:S(2)}) collective-permute-start(f32[8,16,128]{2,1,0:T(8,128)S(1)} %get-tuple-element.18), channel_id=1, source_target_pairs={{0,1},{1,0},{2,3},{3,2},{4,5},{5,4},{6,7},{7,6},{8,9},{9,8},{10,11... | collective-permute-start | bytes 196616 | tf_op jit(solution)/shard_map/ppermute | solution.py:414
  12.7 5.9 %collective-permute-start.1 = (f32[8,16,128]{2,1,0:T(8,128)S(1)}, f32[8,16,128]{2,1,0:T(8,128)S(1)}, u32[]{:S(2)}, u32[]{:S(2)}) collective-permute-start(f32[8,16,128]{2,1,0:T(8,128)S(1)} %get-tuple-element.19), channel_id=1, source_target_pairs={{1,2},{2,1},{3,4},{4,3},{5,6},{6,5},{7,8},{8,7},{9,10},{10,9},{11,... | collective-permute-start | bytes 196616 | tf_op jit(solution)/shard_map/ppermute | solution.py:414
  18.6 12.1 %copy-start.5 = (f32[3,16,16,128]{3,2,1,0:T(8,128)S(1)}, f32[3,16,16,128]{3,2,1,0:T(8,128)}, u32[]{:S(2)}) copy-start(f32[3,16,16,128]{3,2,1,0:T(8,128)} %v.9) | copy-start | bytes 1179652
  18.6 12.1 %copy-start.9 = (f32[16,16,128]{2,1,0:T(8,128)S(1)}, f32[16,16,128]{2,1,0:T(8,128)}, u32[]{:S(2)}) copy-start(f32[16,16,128]{2,1,0:T(8,128)} %b.9) | copy-start | bytes 393220
  20.6 14.3 %copy-start.3 = (f32[6,16,16,128]{3,2,1,0:T(8,128)S(1)}, f32[6,16,16,128]{3,2,1,0:T(8,128)}, u32[]{:S(2)}) copy-start(f32[6,16,16,128]{3,2,1,0:T(8,128)} %s.7) | copy-start | bytes 2359300
  20.6 12.0 %collective-permute-start.2 = (f32[17,16,128]{2,1,0:T(8,128)S(1)}, f32[17,16,128]{2,1,0:T(8,128)S(1)}, u32[]{:S(2)}, u32[]{:S(2)}) collective-permute-start(f32[17,16,128]{2,1,0:T(8,128)S(1)} %get-tuple-element.20), channel_id=1, source_target_pairs={{0,16},{16,0},{32,48},{48,32},{64,80},{80,64},{96,112},{112,96},{1... | collective-permute-start | bytes 417800 | tf_op jit(solution)/shard_map/ppermute | solution.py:414
  24.8 10.1 %copy-start.7 = (f32[3,16,16,128]{3,2,1,0:T(8,128)S(1)}, f32[3,16,16,128]{3,2,1,0:T(8,128)}, u32[]{:S(2)}) copy-start(f32[3,16,16,128]{3,2,1,0:T(8,128)} %v.7) | copy-start | bytes 1179652
  24.8 10.1 %copy-start.10 = (f32[16,16,128]{2,1,0:T(8,128)S(1)}, f32[16,16,128]{2,1,0:T(8,128)}, u32[]{:S(2)}) copy-start(f32[16,16,128]{2,1,0:T(8,128)} %lam.3) | copy-start | bytes 393220
  24.8 10.1 %copy-start.11 = (f32[16,16,128]{2,1,0:T(8,128)S(1)}, f32[16,16,128]{2,1,0:T(8,128)}, u32[]{:S(2)}) copy-start(f32[16,16,128]{2,1,0:T(8,128)} %mu.3) | copy-start | bytes 393220
  24.8 10.1 %collective-permute-start.3 = (f32[17,16,128]{2,1,0:T(8,128)S(1)}, f32[17,16,128]{2,1,0:T(8,128)S(1)}, u32[]{:S(2)}, u32[]{:S(2)}) collective-permute-start(f32[17,16,128]{2,1,0:T(8,128)S(1)} %get-tuple-element.21), channel_id=1, source_target_pairs={{16,32},{32,16},{48,64},{64,48},{80,96},{96,80},{112,128},{128,112... | collective-permute-start | bytes 417800 | tf_op jit(solution)/shard_map/ppermute | solution.py:414
  34.9 3.9 %copy-start.12 = (s32[1,1,8192]{2,1,0:T(1,128)S(1)}, s32[1,1,8192]{2,1,0:T(1,128)}, u32[]{:S(2)}) copy-start(s32[1,1,8192]{2,1,0:T(1,128)} %param.19) | copy-start | bytes 98308
  34.9 3.9 %copy-start.13 = (s32[1,1,8192]{2,1,0:T(1,128)S(1)}, s32[1,1,8192]{2,1,0:T(1,128)}, u32[]{:S(2)}) copy-start(s32[1,1,8192]{2,1,0:T(1,128)} %param.20) | copy-start | bytes 98308
  34.9 3.9 %copy-start.15 = (f32[1,1,8192]{2,1,0:T(1,128)S(1)}, f32[1,1,8192]{2,1,0:T(1,128)}, u32[]{:S(2)}) copy-start(f32[1,1,8192]{2,1,0:T(1,128)} %param.21) | copy-start | bytes 98308
  45.7 13.3 %collective-permute-start.5 = (f32[17,16,128]{2,1,0:T(8,128)S(1)}, f32[17,16,128]{2,1,0:T(8,128)S(1)}, u32[]{:S(2)}, u32[]{:S(2)}) collective-permute-start(f32[17,16,128]{2,1,0:T(8,128)S(1)} %pad_maximum_fusion.1), channel_id=1, source_target_pairs={{16,32},{32,16},{48,64},{64,48},{80,96},{96,80},{112,128},{128,112... | collective-permute-start | bytes 417800 | tf_op jit(solution)/shard_map/ppermute | solution.py:414
  48.9 11.2 %copy-start.16 = (f32[1,2048]{1,0:T(1,128)S(1)}, f32[1,2048]{1,0:T(1,128)}, u32[]{:S(2)}) copy-start(f32[1,2048]{1,0:T(1,128)} %param.23) | copy-start | bytes 24580
  48.9 11.1 %collective-permute-start.4 = (f32[17,16,128]{2,1,0:T(8,128)S(1)}, f32[17,16,128]{2,1,0:T(8,128)S(1)}, u32[]{:S(2)}, u32[]{:S(2)}) collective-permute-start(f32[17,16,128]{2,1,0:T(8,128)S(1)} %pad_maximum_fusion), channel_id=1, source_target_pairs={{0,16},{16,0},{32,48},{48,32},{64,80},{80,64},{96,112},{112,96},{1... | collective-permute-start | bytes 417800 | tf_op jit(solution)/shard_map/ppermute | solution.py:414
  60.6 13.2 %collective-permute-start.7 = (f32[16,128]{1,0:T(8,128)S(1)}, f32[16,128]{1,0:T(8,128)S(1)}, u32[]{:S(2)}, u32[]{:S(2)}) collective-permute-start(f32[16,128]{1,0:T(8,128)S(1)} %get-tuple-element.31.robust), channel_id=1, source_target_pairs={{16,32},{32,16},{48,64},{64,48},{80,96},{96,80},{112,128},{128,112... | collective-permute-start | bytes 24584 | tf_op jit(solution)/shard_map/ppermute | solution.py:414
  62.6 11.2 %collective-permute-start.6 = (f32[16,128]{1,0:T(8,128)S(1)}, f32[16,128]{1,0:T(8,128)S(1)}, u32[]{:S(2)}, u32[]{:S(2)}) collective-permute-start(f32[16,128]{1,0:T(8,128)S(1)} %get-tuple-element.31.robust), channel_id=1, source_target_pairs={{0,16},{16,0},{32,48},{48,32},{64,80},{80,64},{96,112},{112,96},{1... | collective-permute-start | bytes 24584 | tf_op jit(solution)/shard_map/ppermute | solution.py:414
where the time goes:
time: 80.9 us; the launch traced here: 80.4 us
  starting transfers between devices  38.9 us (48%)
  Pallas kernels  27.4 us (34%)
  waiting for transfers between devices  7.16 us (9%)
  local copies, waits for them, and re-layouts  5.23 us (6%)
  between operations  0.93 us (1%)
    ppermute x4, starting transfers between devices, swap(): lax.ppermute(a, axis, pairs(axis, 0))  26.1 us
    ppermute x4, starting transfers between devices, swap(): lax.ppermute(b, axis, pairs(axis, 1))  12.8 us
    pallas_call x1, Pallas kernels, shards(): call(sample_kernel, (shape((48, 128)), shape((3,) + slots)), 7, [pltpu.VM...  6.92 us
    pallas_call x1, Pallas kernels, shards(): call(deposit_kernel, shape((6, 256, 128)), 7, [pltpu.VMEM(slots, jnp.int3...  6.56 us
    ppermute x4, waiting for transfers between devices, swap(): lax.ppermute(b, axis, pairs(axis, 1))  6.19 us
    unnamed x34, local copies, waits for them, and re-layouts  5.23 us
    pallas_call x1, Pallas kernels, shards(): call(functools.partial(step_kernel, 1.0, fields_f, True, True), (speed, t...  3.83 us
    pallas_call x1, Pallas kernels, shards(): call(functools.partial(step_kernel, -1.0, fields_a, False, False), (speed...  3.51 us
  transfers between devices with their start and end apart: 8, of which 3 were waited for; matrix products, arithmetic and copies ran while one was open for 0% of the time, Pallas kernels for 7%

commit v1 on v0

--- a/solution.py
+++ b/solution.py
@@ -118,127 +118,184 @@
         lax.fori_loop(g * depth // 2, (g + 1) * depth // 2, body, 0, unroll=True)
 
 
-def unpack_y_all(even_y, recv_a, recv_b, fields, e_ref, main, pads, m_ref):
+UP = (0, 7, 4, 5, 6, 8, 12, 13, 14, 1, 2, 3, 9, 10, 11)
+DOWN = (1, 2, 7, 3, 6, 9, 10, 11, 14, 0, 4, 5, 8, 12, 13)
+PAIRED = 9
+MSG_ROWS = 24
+
+
+def slot(order, item):
+    at = order.index(item)
+    return 2 * at if at < PAIRED else PAIRED + at
+
+
+def put_rows(acc, order, item, block, first):
+    at = slot(order, item)
+    width = 2 if order.index(item) < PAIRED else 1
+    src = first if width == 2 or first == 0 else first + 1
+    row = iota((8, 128), 0)
+    lo = at % 8
+    moved = pltpu.roll(block, (lo - src) % 8, 0) if (lo - src) % 8 else block
+    acc[at // 8] = jnp.where((row >= lo) & (row < lo + width), moved, acc[at // 8])
+
+
+def get_rows(msg, order, item, first):
+    at = slot(order, item)
+    width = 2 if order.index(item) < PAIRED else 1
+    src = first if width == 2 or first == 0 else first + 1
+    block = msg[8 * (at // 8) : 8 * (at // 8) + 8]
+    turn = (src - at % 8) % 8
+    return pltpu.roll(block, turn, 0) if turn else block
+
+
+def pack_x_kernel(par, s, v, a_s, a_v, b, angle, recv_a, recv_b, out_a, out_b, pv, a_pv, e, a_e, m, a_m):
+    even_y = par[0] == 0
+    even_x = par[1] == 0
     zero = jnp.zeros((16, 128), F32)
-    for k in range(len(fields)):
-        for z in (0, 1, 18, 19):
-            e_ref[k, z] = zero
-    for k in range(len(pads)):
-        for z in (0, 1, 18, 19):
-            m_ref[k, z] = zero
-
-    def body(zz, carry):
+    for ref, n in ((e, 10), (a_e, 9), (m, 3), (a_m, 3)):
+        for k in range(n):
+            for z in (0, 1, 18, 19):
+                ref[k, z] = zero
+
+    def frames(zz, carry):
         low = low_half(iota((16, 128), 1))
         ra = recv_a[zz]
         rb = recv_b[zz]
         before = jnp.where(even_y, rb, ra)
         after = jnp.where(even_y, ra, rb)
-        frames = (
+        both = (
             jnp.where(low, before, pltpu.roll(after, EDGE, 1)),
             jnp.where(low, pltpu.roll(before, 128 - EDGE, 1), after),
         )
-        for sub, frame in enumerate(frames):
+        for sub, frame in enumerate(both):
             z = zz * 2 + sub
-            for k, n in enumerate(fields):
-                e_ref[k, z + 2] = pltpu.roll(frame, (128 - EDGE - 2 * EDGE * n) % 128, 1)
-            for k, n in enumerate(pads):
-                m_ref[k, z + 2] = main[n, z]
-        return carry
-
-    lax.fori_loop(0, 8, body, 0, unroll=UNROLL // 2)
-
-
-def pack_x_kernel(sign, fields, n_extra, par, s, v, b, recv_a, recv_b, *rest):
-    extra = rest[:n_extra]
-    out_a, out_b, e_ref, m_ref = rest[n_extra:]
-    even_x = par[1] == 0
-    unpack_y_all(par[0] == 0, recv_a, recv_b, fields, e_ref, s, (2, 4, 5), m_ref)
+            for n in range(N_Y):
+                value = pltpu.roll(frame, (128 - EDGE - 2 * EDGE * n) % 128, 1)
+                if n < 9:
+                    e[n, z + 2] = value
+                elif n < 18:
+                    a_e[n - 9, z + 2] = value
+                else:
+                    e[9, z + 2] = value
+            for k, n in enumerate((2, 4, 5)):
+                m[k, z + 2] = s[n, z]
+                a_m[k, z + 2] = a_s[n, z]
+        return carry
+
+    lax.fori_loop(0, 8, frames, 0, unroll=UNROLL // 2)
 
     def body(z, carry):
         lane = iota((16, 128), 1)
-        zero = jnp.zeros((16, 128), F32)
-        sxx, syy, sxy, sxz, syz = s[0, z], s[1, z], s[3, z], s[4, z], s[5, z]
-        exx, eyy, exy, exz, eyz = (e_ref[k, z + 2] for k in (0, 1, 3, 4, 5))
         by = b[z]
-        cx = ahead(shift_x, sxx, zero) + behind(shift_y, sxy, exy) + behind_z(m_ref, 1, z)
-        cy = behind(shift_x, sxy, zero) + ahead(shift_y, syy, eyy) + behind_z(m_ref, 2, z)
-        cz = behind(shift_x, sxz, zero) + behind(shift_y, syz, eyz) + ahead_z(m_ref, 0, z)
-        ep = jnp.where(lane < 3, exx, zero)
-        ep = jnp.where(lane >= 125, exx, ep)
-        ep = jnp.where((lane >= 5) & (lane < 11), pltpu.roll(exy, 8, 1), ep)
-        ep = jnp.where((lane >= 13) & (lane < 19), pltpu.roll(exz, 16, 1), ep)
-        items = [v[0, z] + sign * (by * cx), v[1, z] + sign * (by * cy), v[2, z] + sign * (by * cz)]
-        items += [by, sxx, sxy, sxz, ep]
-        up = jnp.concatenate([f[14:16] for f in items], axis=0)
-        down = jnp.concatenate([f[0:2] for f in items], axis=0)
-        out_a[z] = jnp.where(even_x, up, down)
-        out_b[z] = jnp.where(even_x, down, up)
+        up = [jnp.zeros((8, 128), F32)] * 3
+        down = [jnp.zeros((8, 128), F32)] * 3
+        for base, sign, s_ref, v_ref, e_ref, m_ref, out in (
+            (0, 1.0, s, v, e, m, pv),
+            (8, -1.0, a_s, a_v, a_e, a_m, a_pv),
+        ):
+            sxx, syy, sxy, sxz, syz = (s_ref[k, z] for k in (0, 1, 3, 4, 5))
+            exx, eyy, exy, exz, eyz = (e_ref[k, z + 2] for k in (0, 1, 3, 4, 5))
+            cx = ahead(shift_x, sxx, zero) + behind(shift_y, sxy, exy) + behind_z(m_ref, 1, z)
+            cy = behind(shift_x, sxy, zero) + ahead(shift_y, syy, eyy) + behind_z(m_ref, 2, z)
+            cz = behind(shift_x, sxz, zero) + behind(shift_y, syz, eyz) + ahead_z(m_ref, 0, z)
+            ep = jnp.where((lane >= 5) & (lane < 11), pltpu.roll(exy, 8, 1), exx)
+            ep = jnp.where((lane >= 13) & (lane < 19), pltpu.roll(exz, 16, 1), ep)
+            speeds = [v_ref[k, z] + sign * (by * c) for k, c in enumerate((cx, cy, cz))]
+            for k in range(3):
+                out[k, z] = speeds[k]
+            items = speeds + [sxx, sxy, sxz, ep] + ([by] if base == 0 else [])
+            for k, f in enumerate(items):
+                put_rows(up, UP, base + k, f[8:16], 6)
+                put_rows(down, DOWN, base + k, f[0:8], 0)
+        for t in range(3):
+            rows = slice(8 * t, 8 * t + 8)
+            out_a[z, rows] = jnp.where(even_x, up[t], down[t])
+            out_b[z, rows] = jnp.where(even_x, down[t], up[t])
         return carry
 
     lax.fori_loop(0, 16, body, 0, unroll=UNROLL)
-    for k in range(n_extra // 2):
-        out_a[16 + k] = extra[2 * k][...]
-        out_b[16 + k] = extra[2 * k + 1][...]
-
-
-def spread_rows(before, after, k):
-    row = iota((16, 128), 0)
-    left = pltpu.roll(before, (14 - 2 * k) % 16, 0) if k != 7 else before
-    right = pltpu.roll(after, (16 - 2 * k) % 16, 0) if k else after
-    return jnp.where(row < 8, right, left)
-
-
-def step_kernel(
-    sign, fields, with_rates, own_b, par, s, v, b, lam, mu, recv_ya, recv_yb, recv_xa, recv_xb, *rest
-):
-    if own_b:
-        v_out, s_out = rest[:2]
-        rest = rest[2:]
-    else:
-        bxa, bxb, v_out, s_out = rest[:4]
-        rest = rest[4:]
-    if with_rates:
-        r_out = rest[0]
-        rest = rest[1:]
-    e_ref, m_ref, vm_ref, ve_ref, vh_ref = rest
+    for ref in (out_a, out_b):
+        ref[16, 0:16] = angle[...]
+        ref[16, 16:24] = jnp.zeros((8, 128), F32)
+
+
+def frame_kernel(s, a_s, e, a_e, out, a_out):
+    zero = jnp.zeros((16, 128), F32)
+
+    def body(z, carry):
+        be = e[9, z + 2]
+        for sign, s_ref, e_ref, o in ((1.0, s, e, out), (-1.0, a_s, a_e, a_out)):
+            syy, sxy, syz = (s_ref[k, z] for k in (1, 3, 5))
+            exx, eyy, exy, exz, eyz = (e_ref[k, z + 2] for k in (0, 1, 3, 4, 5))
+            cx = ahead(shift_x, exx, zero) + behind(shift_y, exy, sxy) + behind_z(e_ref, 4, z)
+            cy = behind(shift_x, exy, zero) + ahead(shift_y, eyy, syy) + behind_z(e_ref, 5, z)
+            cz = behind(shift_x, exz, zero) + behind(shift_y, eyz, syz) + ahead_z(e_ref, 2, z)
+            for k, c in enumerate((cx, cy, cz)):
+                o[k, z] = e_ref[6 + k, z + 2] + sign * (be * c)
+        return carry
+
+    lax.fori_loop(0, 16, body, 0, unroll=UNROLL)
+
+
+def masked_roll(block, k, low, high):
+    row = iota((8, 128), 0)
+    return jnp.where((row >= low) & (row < high), pltpu.roll(block, k % 8, 0), 0.0)
+
+
+def ahead_first(block):
+    return -C2 * masked_roll(block, 1, 0, 1)
+
+
+def ahead_last(block):
+    return C1 * masked_roll(block, -1, 7, 8) + C2 * masked_roll(block, -2, 6, 8)
+
+
+def behind_first(block):
+    return -C1 * masked_roll(block, 1, 0, 1) - C2 * masked_roll(block, 2, 0, 2)
+
+
+def behind_last(block):
+    return C2 * masked_roll(block, -1, 7, 8)
+
+
+ADDED = ((ahead_first, ahead_last), (behind_first, behind_last), (behind_first, behind_last))
+
+
+def step_kernel(sign, base, par, s, pv, pve, b, be, lam, mu, recv_a, recv_b, v_out, s_out, *rest):
+    r_out = rest[0] if len(rest) == 4 else None
+    vm_ref, ve_ref, vh_ref = rest[-3:]
     even_x = par[1] == 0
-    unpack_y_all(par[0] == 0, recv_ya, recv_yb, fields, e_ref, s, (2, 4, 5), m_ref)
     zero = jnp.zeros((16, 128), F32)
     for k in range(3):
         for z in (0, 1, 18, 19):
             vm_ref[k, z] = zero
 
     def speeds(z, carry):
-        xa = recv_xa[z]
-        xb = recv_xb[z]
+        xa = recv_a[z]
+        xb = recv_b[z]
         before = jnp.where(even_x, xb, xa)
         after = jnp.where(even_x, xa, xb)
-        hx, hy, hz, hb, hxx, hxy, hxz, hp = (spread_rows(before, after, k) for k in range(8))
-        if not own_b:
-            ba = bxa[z]
-            bb = bxb[z]
-            hb = spread_rows(jnp.where(even_x, bb, ba), jnp.where(even_x, ba, bb), 3)
-        hpy = pltpu.roll(hp, 120, 1)
-        hpz = pltpu.roll(hp, 112, 1)
-        sxx, syy, sxy, sxz, syz = s[0, z], s[1, z], s[3, z], s[4, z], s[5, z]
-        exx, eyy, exy, exz, eyz = (e_ref[k, z + 2] for k in (0, 1, 3, 4, 5))
+
+        def halo(item):
+            return (get_rows(before, UP, item, 6), get_rows(after, DOWN, item, 0))
+
+        b_left, b_right = halo(7)
+        p_left, p_right = halo(base + 6)
         by = b[z]
-        be = e_ref[9, z + 2]
-        cx = ahead(shift_x, sxx, hxx) + behind(shift_y, sxy, exy) + behind_z(m_ref, 1, z)
-        cy = behind(shift_x, sxy, hxy) + ahead(shift_y, syy, eyy) + behind_z(m_ref, 2, z)
-        cz = behind(shift_x, sxz, hxz) + behind(shift_y, syz, eyz) + ahead_z(m_ref, 0, z)
-        for k, c in enumerate((cx, cy, cz)):
-            new = v[k, z] + sign * (by * c)
+        bf = be[0, z + 2]
+        for k, (first, last) in enumerate(ADDED):
+            left, right = halo(base + 3 + k)
+            new = pv[k, z] + sign * (by * jnp.concatenate([first(left), last(right)], axis=0))
             vm_ref[k, z + 2] = new
             v_out[k, z] = new
-        cx = ahead(shift_x, exx, hp) + behind(shift_y, exy, sxy) + behind_z(e_ref, 4, z)
-        cy = behind(shift_x, exy, hpy) + ahead(shift_y, eyy, syy) + behind_z(e_ref, 5, z)
-        cz = behind(shift_x, exz, hpz) + behind(shift_y, eyz, syz) + ahead_z(e_ref, 2, z)
-        for k, c in enumerate((cx, cy, cz)):
-            ve_ref[k, z] = e_ref[6 + k, z + 2] + sign * (be * c)
-        vh_ref[0, z] = hx + sign * (hb * ahead(shift_x, zero, sxx))
-        vh_ref[1, z] = hy + sign * (hb * behind(shift_x, zero, sxy))
-        vh_ref[2, z] = hz + sign * (hb * behind(shift_x, zero, sxz))
+            turn = (128 - 8 * k) % 128
+            e_left = pltpu.roll(p_left, turn, 1) if turn else p_left
+            e_right = pltpu.roll(p_right, turn, 1) if turn else p_right
+            ve_ref[k, z] = pve[k, z] + sign * (bf * jnp.concatenate([first(e_left), last(e_right)], axis=0))
+            v_left, v_right = halo(base + k)
+            f = s[(0, 3, 4)[k], z]
+            vh_ref[k, z, 0:8] = v_right + sign * (b_right * first(f[8:16]))
+            vh_ref[k, z, 8:16] = v_left + sign * (b_left * last(f[0:8]))
         return carry
 
     lax.fori_loop(0, 16, speeds, 0, unroll=UNROLL)
@@ -258,7 +315,7 @@
         m2 = 2.0 * m
         for k, c in enumerate((volume + m2 * r0, volume + m2 * r1, volume + m2 * r2, m * r3, m * r4, m * r5)):
             s_out[k, z] = s[k, z] + sign * c
-        if with_rates:
+        if r_out is not None:
             r_out[0, z] = r0
             r_out[1, z] = r1
             r_out[2, z] = r3
@@ -321,11 +378,13 @@
     return jnp.concatenate(pieces(rows.T, 3), axis=1)
 
 
-def sample_kernel(par, cell, chan_raw, weight, angle_a, angle, angle_b, rates, part, trig, chan, table, rows, vals):
+def sample_kernel(
+    par, cell, chan_raw, weight, recv_a, angle, recv_b, rates, part, part_a, part_b, trig, chan, table, rows, vals
+):
     chan[...] = chan_raw[...] - par[2]
     even_x = par[1] == 0
-    aa = angle_a[...]
-    ab = angle_b[...]
+    aa = recv_a[16, 0:16]
+    ab = recv_b[16, 0:16]
     angles = jnp.concatenate([jnp.where(even_x, ab, aa), angle[...], jnp.where(even_x, aa, ab)], axis=0)
     ang = channel_table(angles)
     for k in range(3):
@@ -365,7 +424,10 @@
         return acc + dot_nt(a.astype(BF16), one_hot(c & 127, 128))
 
     acc = lax.fori_loop(0, 8192 // CHUNK, scatter, jnp.zeros((144, 128), F32))
-    part[...] = acc[0:48] + acc[48:96] + acc[96:144]
+    total = acc[0:48] + acc[48:96] + acc[96:144]
+    part[...] = total[16:32]
+    part_a[...] = jnp.where(even_x, total[32:48], total[0:16])
+    part_b[...] = jnp.where(even_x, total[0:16], total[32:48])
 
 
 def deposit_kernel(par, cell, chan_raw, trig, robust_a, robust, robust_b, pulled, out, chan, vals, acc):
@@ -414,14 +476,14 @@
     return (lax.ppermute(a, axis, pairs(axis, 0)), lax.ppermute(b, axis, pairs(axis, 1)))
 
 
-def call(kernel, outs, n_in, scratch, name, space=pltpu.VMEM):
+def call(kernel, outs, n_in, scratch, name, space=pltpu.VMEM, limit=VMEM_LIMIT):
     return pl.pallas_call(
         kernel,
         out_shape=outs,
         in_specs=[pl.BlockSpec(memory_space=pltpu.SMEM)] + [pl.BlockSpec(memory_space=space)] * n_in,
         out_specs=jax.tree.map(lambda _: whole(), outs),
         scratch_shapes=scratch,
-        compiler_params=pltpu.CompilerParams(vmem_limit_bytes=VMEM_LIMIT),
+        compiler_params=pltpu.CompilerParams(vmem_limit_bytes=limit),
         name=name,
     )
 
@@ -444,7 +506,6 @@
     gx = lax.axis_index("gx")
     gy = lax.axis_index("gy")
     par = jnp.stack([gy % 2, gx % 2, (gx - 1) * owned]).astype(jnp.int32)
-    even_x = gx % 2 == 0
     slots = (ROWS, 128)
     cell = gauge_cell.reshape(slots)
     chan = gauge_channel.reshape(slots)
@@ -460,39 +521,43 @@
         + [pltpu.SemaphoreType.DMA((Y_GROUPS, 5))],
         "pack_y",
         pltpu.HBM,
+        60 * 1024 * 1024,
     )(
         par, stress, velocity, adj_stress, adj_velocity, buoyancy
     )
     ya, yb = swap(msg_a, msg_b, "gy")
 
-    e_scratch = pltpu.VMEM((10, 20, 16, 128), F32)
-    m_scratch = pltpu.VMEM((3, 20, 16, 128), F32)
-    fields_f = tuple(range(9)) + (18,)
-    fields_a = tuple(range(9, 18)) + (18,)
-    msg = shape((17, 16, 128))
-    fa, fb = call(
-        functools.partial(pack_x_kernel, 1.0, fields_f, 2), (msg, msg), 7, [e_scratch, m_scratch], "pack_x"
-    )(par, stress, velocity, buoyancy, ya, yb, angle, angle)
-    fa, fb = swap(fa, fb, "gx")
-    msg = shape((16, 16, 128))
-    aa, ab = call(
-        functools.partial(pack_x_kernel, -1.0, fields_a, 0), (msg, msg), 5, [e_scratch, m_scratch], "pack_x_adj"
-    )(par, adj_stress, adj_velocity, buoyancy, ya, yb)
-
     speed = shape((3, 16, 16, 128))
     tensor = shape((6, 16, 16, 128))
+    msg = shape((17, MSG_ROWS, 128))
+    m_scratch = pltpu.VMEM((3, 20, 16, 128), F32)
+    xa, xb, part_v, adj_part_v, edge, adj_edge = call(
+        pack_x_kernel,
+        (msg, msg, speed, speed, shape((10, 20, 16, 128)), shape((9, 20, 16, 128))),
+        8,
+        [m_scratch, m_scratch],
+        "pack_x",
+    )(par, stress, velocity, adj_stress, adj_velocity, buoyancy, angle, ya, yb)
+    xa, xb = swap(xa, xb, "gx")
+    frame_v, adj_frame_v = pl.pallas_call(
+        frame_kernel,
+        out_shape=(speed, speed),
+        in_specs=[whole()] * 4,
+        out_specs=(whole(), whole()),
+        compiler_params=pltpu.CompilerParams(vmem_limit_bytes=VMEM_LIMIT),
+        name="frame",
+    )(stress, adj_stress, edge, adj_edge)
+
     v_scratch = [pltpu.VMEM((3, 20, 16, 128), F32)] + [pltpu.VMEM((3, 16, 16, 128), F32)] * 2
+    buoyancy_edge = edge[9:10]
     velocity_next, stress_next, rates = call(
-        functools.partial(step_kernel, 1.0, fields_f, True, True),
-        (speed, tensor, speed),
-        9,
-        [e_scratch, m_scratch] + v_scratch,
-        "step",
-    )(par, stress, velocity, buoyancy, lame_lambda, shear_modulus, ya, yb, fa, fb)
-
-    part, trig = call(
+        functools.partial(step_kernel, 1.0, 0), (speed, tensor, speed), 9, v_scratch, "step"
+    )(par, stress, part_v, frame_v, buoyancy, buoyancy_edge, lame_lambda, shear_modulus, xa, xb)
+
+    tile = shape((16, 128))
+    part, part_a, part_b, trig = call(
         sample_kernel,
-        (shape((48, 128)), shape((3,) + slots)),
+        (tile, tile, tile, shape((3,) + slots)),
         7,
         [
             pltpu.VMEM(slots, jnp.int32),
@@ -501,25 +566,17 @@
             pltpu.VMEM((3,) + slots, F32),
         ],
         "sample",
-    )(par, cell, chan, weight, fa[16], angle, fb[16], rates.reshape(3, 256, 128))
-
-    to_after = part[32:48]
-    to_before = part[0:16]
-    send_a = jnp.concatenate([aa, jnp.where(even_x, to_after, to_before)[None]], axis=0)
-    send_b = jnp.concatenate([ab, jnp.where(even_x, to_before, to_after)[None]], axis=0)
-    aa, ab = swap(send_a, send_b, "gx")
-    predicted = part[16:32] + aa[16] + ab[16]
+    )(par, cell, chan, weight, xa, angle, xb, rates.reshape(3, 256, 128))
+
+    part_a, part_b = swap(part_a, part_b, "gx")
+    adj_velocity_next, pulled = call(
+        functools.partial(step_kernel, -1.0, 8), (speed, tensor), 9, v_scratch, "step_adj"
+    )(par, adj_stress, adj_part_v, adj_frame_v, buoyancy, buoyancy_edge, lame_lambda, shear_modulus, xa, xb)
+
+    predicted = part + part_a + part_b
     misfit = predicted - observed.reshape(16, 128)
     robust = misfit / jnp.sqrt(HUBER_SQUARE + misfit * misfit)
     robust_a, robust_b = swap(robust, robust, "gx")
-
-    adj_velocity_next, pulled = call(
-        functools.partial(step_kernel, -1.0, fields_a, False, False),
-        (speed, tensor),
-        11,
-        [e_scratch, m_scratch] + v_scratch,
-        "step_adj",
-    )(par, adj_stress, adj_velocity, buoyancy, lame_lambda, shear_modulus, ya, yb, aa, ab, fa, fb)
 
     adj_stress_next = call(
         deposit_kernel,

time: 80.9 us -> 75.9 us (0.938)
  the two profiles are of different devices: /device:TPU:31 before, /device:TPU:38 now
where the time goes in v1:
time: 75.9 us; the launch traced here: 75.6 us
  starting transfers between devices  33.5 us (44%)
  Pallas kernels  26 us (34%)
  waiting for transfers between devices  14 us (18%)
  other arithmetic  1.19 us (2%)
  between operations  0.9 us (1%)
    ppermute x4, starting transfers between devices, swap(): lax.ppermute(b, axis, pairs(axis, 1))  23.5 us
    ppermute x4, waiting for transfers between devices, swap(): lax.ppermute(b, axis, pairs(axis, 1))  13.4 us
    ppermute x4, starting transfers between devices, swap(): lax.ppermute(a, axis, pairs(axis, 0))  10 us
    pallas_call x1, Pallas kernels, shards(): call(sample_kernel, (tile, tile, tile, shape((3,) + slots)), 7, [pltpu.VM...  6.88 us
    pallas_call x1, Pallas kernels, shards(): call(deposit_kernel, shape((6, 256, 128)), 7, [pltpu.VMEM(slots, jnp.int3...  6.56 us
    pallas_call x1, Pallas kernels, shards(): call(pack_y_kernel, (slab, slab), 5, [pltpu.VMEM(f.shape, F32) for f in (...  4.35 us
    pallas_call x1, Pallas kernels, shards(): call(pack_x_kernel, (msg, msg, speed, speed, shape((10, 20, 16, 128)), sh...  3.02 us
    pallas_call x1, Pallas kernels, shards(): call(functools.partial(step_kernel, 1.0, 0), (speed, tensor, speed), 9, v...  2.33 us
  transfers between devices with their start and end apart: 8, of which 5 were waited for; matrix products, arithmetic and copies ran while one was open for 0% of the time, Pallas kernels for 4%

profile of v1, /device:TPU:38, one launch (start us, length us, event | category | flops | bytes accessed | tf_op | source)
XLA Modules:
  0.0 75.6 jit_solution(3102040784467280705)
XLA Ops:
  0.6 0.0 copy-start.3
  0.6 0.0 copy-start
  0.7 0.0 copy-start.4
  0.7 0.0 copy-start.1
  0.7 0.0 copy-start.2
  0.7 0.0 copy-start.9
  0.7 0.6 pad_add_fusion.par
  1.3 4.3 %pack_y.1 = (f32[8,16,128]{2,1,0:T(8,128)}, f32[8,16,128]{2,1,0:T(8,128)}) custom-call(s32[3]{0:T(128)} %pad_add_fusion.par, f32[6,16,16,128]{3,2,1,0:T(8,128)} %s.8, f32[3,16,16,128]{3,2,1,0:T(8,128)} %v.3, f32[6,16,16,128]{3,2,1,0:T(8,128)} %s.9, f32[3,16,16,128]{3,2,1,0:T(8,128)} %a_v.3, f32[16,16,128]{2,1,0:T(8,128)} %b.7), custom_call_target="tpu_custom_call" | custom-call | tf_op jit(solution)/shard_map/pack_y/pallas_call | solution.py:516
  5.7 4.3 %collective-permute-start = (f32[8,16,128]{2,1,0:T(8,128)}, f32[8,16,128]{2,1,0:T(8,128)S(1)}, u32[]{:S(2)}, u32[]{:S(2)}) collective-permute-start(f32[8,16,128]{2,1,0:T(8,128)} %get-tuple-element.24), channel_id=1, source_target_pairs={{0,1},{1,0},{2,3},{3,2},{4,5},{5,4},{6,7},{7,6},{8,9},{9,8},{10,11... | collective-permute-start | bytes 196616 | tf_op jit(solution)/shard_map/ppermute | solution.py:476
  10.0 1.9 %collective-permute-start.1 = (f32[8,16,128]{2,1,0:T(8,128)}, f32[8,16,128]{2,1,0:T(8,128)S(1)}, u32[]{:S(2)}, u32[]{:S(2)}) collective-permute-start(f32[8,16,128]{2,1,0:T(8,128)} %get-tuple-element.25), channel_id=1, source_target_pairs={{1,2},{2,1},{3,4},{4,3},{5,6},{6,5},{7,8},{8,7},{9,10},{10,9},{11,... | collective-permute-start | bytes 196616 | tf_op jit(solution)/shard_map/ppermute | solution.py:476
  11.9 0.5 collective-permute-done.recv_a
  12.4 6.0 %collective-permute-done.1.recv_b = f32[8,16,128]{2,1,0:T(8,128)S(1)} collective-permute-done((f32[8,16,128]{2,1,0:T(8,128)}, f32[8,16,128]{2,1,0:T(8,128)S(1)}, u32[]{:S(2)}, u32[]{:S(2)}) %collective-permute-start.1) | collective-permute-done | bytes 65568 | tf_op jit(solution)/shard_map/ppermute | solution.py:476
  18.4 0.0 copy-done.3
  18.4 0.0 copy-done
  18.4 0.0 copy-done.4
  18.4 0.0 copy-done.1
  18.5 0.0 copy-done.2
  18.5 0.0 copy-done.9
  18.5 0.0 copy-done.11
  18.5 3.0 %pack_x.1 = (f32[17,24,128]{2,1,0:T(8,128)S(1)}, f32[17,24,128]{2,1,0:T(8,128)S(1)}, f32[3,16,16,128]{3,2,1,0:T(8,128)S(1)}, f32[3,16,16,128]{3,2,1,0:T(8,128)S(...) custom-call(s32[3]{0:T(128)S(1)} %copy-done.11, f32[6,16,16,128]{3,2,1,0:T(8,128)S(1)} %copy-done, ...), custom_call_target="tpu_custom_call" | custom-call | tf_op jit(solution)/shard_map/pack_x/pallas_call | solution.py:534
  21.5 1.9 %collective-permute-start.2 = (f32[17,24,128]{2,1,0:T(8,128)S(1)}, f32[17,24,128]{2,1,0:T(8,128)S(1)}, u32[]{:S(2)}, u32[]{:S(2)}) collective-permute-start(f32[17,24,128]{2,1,0:T(8,128)S(1)} %get-tuple-element.30), channel_id=1, source_target_pairs={{0,16},{16,0},{32,48},{48,32},{64,80},{80,64},{96,112},{112,96},{1... | collective-permute-start | bytes 626696 | tf_op jit(solution)/shard_map/ppermute | solution.py:476
  23.4 10.4 %collective-permute-start.3 = (f32[17,24,128]{2,1,0:T(8,128)S(1)}, f32[17,24,128]{2,1,0:T(8,128)S(1)}, u32[]{:S(2)}, u32[]{:S(2)}) collective-permute-start(f32[17,24,128]{2,1,0:T(8,128)S(1)} %get-tuple-element.31), channel_id=1, source_target_pairs={{16,32},{32,16},{48,64},{64,48},{80,96},{96,80},{112,128},{128,112... | collective-permute-start | bytes 626696 | tf_op jit(solution)/shard_map/ppermute | solution.py:476
  33.9 0.0 copy-start.5
  33.9 0.0 copy-start.6
  33.9 0.9 %frame.1 = (f32[3,16,16,128]{3,2,1,0:T(8,128)S(1)}, f32[3,16,16,128]{3,2,1,0:T(8,128)S(1)}) custom-call(f32[6,16,16,128]{3,2,1,0:T(8,128)S(1)} %copy-done, f32[6,16,16,128]{3,2,1,0:T(8,128)S(1)} %copy-done.1, f32[10,20,16,128]{3,2,1,0:T(8,128)S(1)} %get-tuple-element.27.e, f32[9,20,16,128]{3,2,1,0:T(8,128)S(1)} %get-tuple-element.28.a_e), custom_call_target="tpu_custom_call" | custom-call | tf_op jit(solution)/shard_map/frame/pallas_call | solution.py:542
  34.8 0.0 copy-start.7
  34.8 0.0 copy-start.8
  34.8 0.0 copy-start.10
  34.8 0.0 collective-permute-done.2.recv_a
  34.8 4.6 %collective-permute-done.3.recv_b = f32[17,24,128]{2,1,0:T(8,128)S(1)} collective-permute-done((f32[17,24,128]{2,1,0:T(8,128)S(1)}, f32[17,24,128]{2,1,0:T(8,128)S(1)}, u32[]{:S(2)}, u32[]{:S(2)}) %collective-permute-start.3) | collective-permute-done | bytes 208928 | tf_op jit(solution)/shard_map/ppermute | solution.py:476
  39.4 0.0 copy-done.5
  39.4 0.0 copy-done.6
  39.4 2.3 %step.1 = (f32[3,16,16,128]{3,2,1,0:T(8,128)}, f32[6,16,16,128]{3,2,1,0:T(8,128)}, f32[3,16,16,128]{3,2,1,0:T(8,128)S(1)}) custom-call(s32[3]{0:T(128)S(1)} %copy-done.11, f32[6,16,16,128]{3,2,1,0:T(8,128)S(1)} %copy-done, f32[3,16,16,128]{3,2,1,0:T(8,128)S(1)} %get-tuple-element.26.pv, f32[3,16,16,128]{3,2,1,0:T(8,128)S(1)} %get-tuple-element.29.pve, ...), custom_call_target="tpu_custom_call" | custom-call | tf_op jit(solution)/shard_map/step/pallas_call | solution.py:553
  41.7 0.0 copy-done.7
  41.7 0.0 copy-done.8
  41.8 0.0 copy-done.10
  41.8 6.9 %sample.1 = (f32[16,128]{1,0:T(8,128)S(1)}, f32[16,128]{1,0:T(8,128)S(1)}, f32[16,128]{1,0:T(8,128)S(1)}, f32[3,64,128]{2,1,0:T(8,128)S(1)}) custom-call(s32[3]{0:T(128)S(1)} %copy-done.11, s32[64,128]{1,0:T(8,128)S(1)} %bitcast.14, s32[64,128]{1,0:T(8,128)S(1)} %bitcast.16, f32[64,128]{1,0:T(8,128)S(1)} %bitcast.20, ...), custom_call_target="tpu_custom_call" | custom-call | tf_op jit(solution)/shard_map/sample/pallas_call | solution.py:558
  48.6 1.9 %collective-permute-start.4 = (f32[16,128]{1,0:T(8,128)S(1)}, f32[16,128]{1,0:T(8,128)S(1)}, u32[]{:S(2)}, u32[]{:S(2)}) collective-permute-start(f32[16,128]{1,0:T(8,128)S(1)} %get-tuple-element.36), channel_id=1, source_target_pairs={{0,16},{16,0},{32,48},{48,32},{64,80},{80,64},{96,112},{112,96},{1... | collective-permute-start | bytes 24584 | tf_op jit(solution)/shard_map/ppermute | solution.py:476
  50.6 5.6 %collective-permute-start.5 = (f32[16,128]{1,0:T(8,128)S(1)}, f32[16,128]{1,0:T(8,128)S(1)}, u32[]{:S(2)}, u32[]{:S(2)}) collective-permute-start(f32[16,128]{1,0:T(8,128)S(1)} %get-tuple-element.37), channel_id=1, source_target_pairs={{16,32},{32,16},{48,64},{64,48},{80,96},{96,80},{112,128},{128,112... | collective-permute-start | bytes 24584 | tf_op jit(solution)/shard_map/ppermute | solution.py:476
  56.2 0.0 collective-permute-done.4
  56.2 2.4 %collective-permute-done.5 = f32[16,128]{1,0:T(8,128)S(1)} collective-permute-done((f32[16,128]{1,0:T(8,128)S(1)}, f32[16,128]{1,0:T(8,128)S(1)}, u32[]{:S(2)}, u32[]{:S(2)}) %collective-permute-start.5) | collective-permute-done | bytes 8224 | tf_op jit(solution)/shard_map/ppermute | solution.py:476
  58.6 0.6 rsqrt_multiply_fusion
  59.2 1.9 %collective-permute-start.6 = (f32[16,128]{1,0:T(8,128)S(1)}, f32[16,128]{1,0:T(8,128)S(1)}, u32[]{:S(2)}, u32[]{:S(2)}) collective-permute-start(f32[16,128]{1,0:T(8,128)S(1)} %get-tuple-element.43.robust), channel_id=1, source_target_pairs={{0,16},{16,0},{32,48},{48,32},{64,80},{80,64},{96,112},{112,96},{1... | collective-permute-start | bytes 24584 | tf_op jit(solution)/shard_map/ppermute | solution.py:476
  61.1 5.6 %collective-permute-start.7 = (f32[16,128]{1,0:T(8,128)S(1)}, f32[16,128]{1,0:T(8,128)S(1)}, u32[]{:S(2)}, u32[]{:S(2)}) collective-permute-start(f32[16,128]{1,0:T(8,128)S(1)} %get-tuple-element.43.robust), channel_id=1, source_target_pairs={{16,32},{32,16},{48,64},{64,48},{80,96},{96,80},{112,128},{128,112... | collective-permute-start | bytes 24584 | tf_op jit(solution)/shard_map/ppermute | solution.py:476
  66.7 2.0 %step_adj.1 = (f32[3,16,16,128]{3,2,1,0:T(8,128)}, f32[6,16,16,128]{3,2,1,0:T(8,128)S(1)}) custom-call(s32[3]{0:T(128)S(1)} %copy-done.11, f32[6,16,16,128]{3,2,1,0:T(8,128)S(1)} %copy-done.1, f32[3,16,16,128]{3,2,1,0:T(8,128)S(1)} %get-tuple-element.38.pv, f32[3,16,16,128]{3,2,1,0:T(8,128)S(1)} %get-tuple-element.39.pve, f32[16,16,128]{2,1,0:T(8,128)S(1)} %copy-done.2, ...), custom_call_target="tpu_custom_call" | custom-call | tf_op jit(solution)/shard_map/step_adj/pallas_call | solution.py:572
  68.6 0.0 collective-permute-done.6.robust_a
  68.6 0.4 collective-permute-done.7.robust_b
  69.1 6.6 %deposit.1 = f32[6,256,128]{2,1,0:T(8,128)} custom-call(s32[3]{0:T(128)S(1)} %copy-done.11, s32[64,128]{1,0:T(8,128)S(1)} %bitcast.15, s32[64,128]{1,0:T(8,128)S(1)} %bitcast.17, f32[3,64,128]{2,1,0:T(8,128)S(1)} %get-tuple-element.41.trig, f32[16,128]{1,0:T(8,128)S(1)} %collective-permute-done.6.robust_a, f32[16,128]{1,0:T(8,128)S(1)} %get-tuple-element.43.robust, ...), custom_call_target="tpu_custom_call" | custom-call | tf_op jit(solution)/shard_map/deposit/pallas_call | solution.py:581
  (4 shorter events, 0.0 us)
Async XLA Ops:
  0.6 17.8 %copy-start.3 = (f32[3,16,16,128]{3,2,1,0:T(8,128)S(1)}, f32[3,16,16,128]{3,2,1,0:T(8,128)}, u32[]{:S(2)}) copy-start(f32[3,16,16,128]{3,2,1,0:T(8,128)} %v.3) | copy-start | bytes 1179652
  0.6 17.8 %copy-start = (f32[6,16,16,128]{3,2,1,0:T(8,128)S(1)}, f32[6,16,16,128]{3,2,1,0:T(8,128)}, u32[]{:S(2)}) copy-start(f32[6,16,16,128]{3,2,1,0:T(8,128)} %s.8) | copy-start | bytes 2359300
  0.7 17.8 %copy-start.4 = (f32[3,16,16,128]{3,2,1,0:T(8,128)S(1)}, f32[3,16,16,128]{3,2,1,0:T(8,128)}, u32[]{:S(2)}) copy-start(f32[3,16,16,128]{3,2,1,0:T(8,128)} %a_v.3) | copy-start | bytes 1179652
  0.7 17.8 %copy-start.1 = (f32[6,16,16,128]{3,2,1,0:T(8,128)S(1)}, f32[6,16,16,128]{3,2,1,0:T(8,128)}, u32[]{:S(2)}) copy-start(f32[6,16,16,128]{3,2,1,0:T(8,128)} %s.9) | copy-start | bytes 2359300
  0.7 17.8 %copy-start.2 = (f32[16,16,128]{2,1,0:T(8,128)S(1)}, f32[16,16,128]{2,1,0:T(8,128)}, u32[]{:S(2)}) copy-start(f32[16,16,128]{2,1,0:T(8,128)} %b.7) | copy-start | bytes 393220
  0.7 17.8 %copy-start.9 = (f32[1,2048]{1,0:T(1,128)S(1)}, f32[1,2048]{1,0:T(1,128)}, u32[]{:S(2)}) copy-start(f32[1,2048]{1,0:T(1,128)} %param.22) | copy-start | bytes 24580
  1.3 17.2 %copy-start.11 = (s32[3]{0:T(128)S(1)}, s32[3]{0:T(128)}, u32[]{:S(2)}) copy-start(s32[3]{0:T(128)} %pad_add_fusion.par) | copy-start | bytes 40
  5.7 6.7 %collective-permute-start = (f32[8,16,128]{2,1,0:T(8,128)}, f32[8,16,128]{2,1,0:T(8,128)S(1)}, u32[]{:S(2)}, u32[]{:S(2)}) collective-permute-start(f32[8,16,128]{2,1,0:T(8,128)} %get-tuple-element.24), channel_id=1, source_target_pairs={{0,1},{1,0},{2,3},{3,2},{4,5},{5,4},{6,7},{7,6},{8,9},{9,8},{10,11... | collective-permute-start | bytes 196616 | tf_op jit(solution)/shard_map/ppermute | solution.py:476
  10.0 8.5 %collective-permute-start.1 = (f32[8,16,128]{2,1,0:T(8,128)}, f32[8,16,128]{2,1,0:T(8,128)S(1)}, u32[]{:S(2)}, u32[]{:S(2)}) collective-permute-start(f32[8,16,128]{2,1,0:T(8,128)} %get-tuple-element.25), channel_id=1, source_target_pairs={{1,2},{2,1},{3,4},{4,3},{5,6},{6,5},{7,8},{8,7},{9,10},{10,9},{11,... | collective-permute-start | bytes 196616 | tf_op jit(solution)/shard_map/ppermute | solution.py:476
  21.5 13.3 %collective-permute-start.2 = (f32[17,24,128]{2,1,0:T(8,128)S(1)}, f32[17,24,128]{2,1,0:T(8,128)S(1)}, u32[]{:S(2)}, u32[]{:S(2)}) collective-permute-start(f32[17,24,128]{2,1,0:T(8,128)S(1)} %get-tuple-element.30), channel_id=1, source_target_pairs={{0,16},{16,0},{32,48},{48,32},{64,80},{80,64},{96,112},{112,96},{1... | collective-permute-start | bytes 626696 | tf_op jit(solution)/shard_map/ppermute | solution.py:476
  23.4 16.0 %collective-permute-start.3 = (f32[17,24,128]{2,1,0:T(8,128)S(1)}, f32[17,24,128]{2,1,0:T(8,128)S(1)}, u32[]{:S(2)}, u32[]{:S(2)}) collective-permute-start(f32[17,24,128]{2,1,0:T(8,128)S(1)} %get-tuple-element.31), channel_id=1, source_target_pairs={{16,32},{32,16},{48,64},{64,48},{80,96},{96,80},{112,128},{128,112... | collective-permute-start | bytes 626696 | tf_op jit(solution)/shard_map/ppermute | solution.py:476
  33.9 5.5 %copy-start.5 = (f32[16,16,128]{2,1,0:T(8,128)S(1)}, f32[16,16,128]{2,1,0:T(8,128)}, u32[]{:S(2)}) copy-start(f32[16,16,128]{2,1,0:T(8,128)} %lam.3) | copy-start | bytes 393220
  33.9 5.5 %copy-start.6 = (f32[16,16,128]{2,1,0:T(8,128)S(1)}, f32[16,16,128]{2,1,0:T(8,128)}, u32[]{:S(2)}) copy-start(f32[16,16,128]{2,1,0:T(8,128)} %mu.3) | copy-start | bytes 393220
  34.8 7.0 %copy-start.7 = (s32[1,1,8192]{2,1,0:T(1,128)S(1)}, s32[1,1,8192]{2,1,0:T(1,128)}, u32[]{:S(2)}) copy-start(s32[1,1,8192]{2,1,0:T(1,128)} %param.19) | copy-start | bytes 98308
  34.8 7.0 %copy-start.8 = (s32[1,1,8192]{2,1,0:T(1,128)S(1)}, s32[1,1,8192]{2,1,0:T(1,128)}, u32[]{:S(2)}) copy-start(s32[1,1,8192]{2,1,0:T(1,128)} %param.20) | copy-start | bytes 98308
  34.8 6.9 %copy-start.10 = (f32[1,1,8192]{2,1,0:T(1,128)S(1)}, f32[1,1,8192]{2,1,0:T(1,128)}, u32[]{:S(2)}) copy-start(f32[1,1,8192]{2,1,0:T(1,128)} %param.21) | copy-start | bytes 98308
  39.4 19.1 %copy-start.12 = (f32[1,2048]{1,0:T(1,128)S(1)}, f32[1,2048]{1,0:T(1,128)}, u32[]{:S(2)}) copy-start(f32[1,2048]{1,0:T(1,128)} %param.23) | copy-start | bytes 24580
  48.6 7.5 %collective-permute-start.4 = (f32[16,128]{1,0:T(8,128)S(1)}, f32[16,128]{1,0:T(8,128)S(1)}, u32[]{:S(2)}, u32[]{:S(2)}) collective-permute-start(f32[16,128]{1,0:T(8,128)S(1)} %get-tuple-element.36), channel_id=1, source_target_pairs={{0,16},{16,0},{32,48},{48,32},{64,80},{80,64},{96,112},{112,96},{1... | collective-permute-start | bytes 24584 | tf_op jit(solution)/shard_map/ppermute | solution.py:476
  50.6 8.0 %collective-permute-start.5 = (f32[16,128]{1,0:T(8,128)S(1)}, f32[16,128]{1,0:T(8,128)S(1)}, u32[]{:S(2)}, u32[]{:S(2)}) collective-permute-start(f32[16,128]{1,0:T(8,128)S(1)} %get-tuple-element.37), channel_id=1, source_target_pairs={{16,32},{32,16},{48,64},{64,48},{80,96},{96,80},{112,128},{128,112... | collective-permute-start | bytes 24584 | tf_op jit(solution)/shard_map/ppermute | solution.py:476
  59.2 9.5 %collective-permute-start.6 = (f32[16,128]{1,0:T(8,128)S(1)}, f32[16,128]{1,0:T(8,128)S(1)}, u32[]{:S(2)}, u32[]{:S(2)}) collective-permute-start(f32[16,128]{1,0:T(8,128)S(1)} %get-tuple-element.43.robust), channel_id=1, source_target_pairs={{0,16},{16,0},{32,48},{48,32},{64,80},{80,64},{96,112},{112,96},{1... | collective-permute-start | bytes 24584 | tf_op jit(solution)/shard_map/ppermute | solution.py:476
  61.1 8.0 %collective-permute-start.7 = (f32[16,128]{1,0:T(8,128)S(1)}, f32[16,128]{1,0:T(8,128)S(1)}, u32[]{:S(2)}, u32[]{:S(2)}) collective-permute-start(f32[16,128]{1,0:T(8,128)S(1)} %get-tuple-element.43.robust), channel_id=1, source_target_pairs={{16,32},{32,16},{48,64},{64,48},{80,96},{96,80},{112,128},{128,112... | collective-permute-start | bytes 24584 | tf_op jit(solution)/shard_map/ppermute | solution.py:476

commit v2 on v1

--- a/solution.py
+++ b/solution.py
@@ -17,7 +17,7 @@
 N_Y = 19
 EDGE = 3
 Y_GROUPS = 2
-UNROLL = 8
+UNROLL = 16
 
 
 def whole():
@@ -64,20 +64,12 @@
     return C1 * (ref[k, z + 2] - ref[k, z + 1]) + C2 * (ref[k, z + 3] - ref[k, z])
 
 
-def parity(axis):
-    return lax.axis_index(axis) % 2
-
-
-def side(par_row, first, second):
-    return jnp.where(par_row == 0, first, second)
-
-
 def low_half(lane):
     return lane % (2 * EDGE) < EDGE
 
 
-def pack_y_kernel(par, s, v, a_s, a_v, b, out_a, out_b, s_ref, v_ref, as_ref, av_ref, b_ref, sems):
-    even = par[0] == 0
+def pack_y_kernel(s, v, a_s, a_v, b, out_a, out_b, s_ref, v_ref, as_ref, av_ref, b_ref, sems):
+    odd = lax.axis_index("gy") % 2 == 1
     hbm = (s, v, a_s, a_v)
     vmem = (s_ref, v_ref, as_ref, av_ref)
     depth = 16 // Y_GROUPS
@@ -108,8 +100,8 @@
         second = packed(2 * zz + 1)
         up = jnp.where(low, first, pltpu.roll(second, EDGE, 1))
         down = jnp.where(low, pltpu.roll(first, 128 - EDGE, 1), second)
-        out_a[zz] = jnp.where(even, up, down)
-        out_b[zz] = jnp.where(even, down, up)
+        out_a[zz] = jnp.where(odd, up, down)
+        out_b[zz] = jnp.where(odd, down, up)
         return carry
 
     for g in range(Y_GROUPS):
@@ -148,9 +140,9 @@
     return pltpu.roll(block, turn, 0) if turn else block
 
 
-def pack_x_kernel(par, s, v, a_s, a_v, b, angle, recv_a, recv_b, out_a, out_b, pv, a_pv, e, a_e, m, a_m):
-    even_y = par[0] == 0
-    even_x = par[1] == 0
+def pack_x_kernel(s, v, a_s, a_v, b, angle, recv_a, recv_b, out_a, out_b, pv, a_pv, e, a_e, m, a_m):
+    odd_y = lax.axis_index("gy") % 2 == 1
+    odd_x = lax.axis_index("gx") % 2 == 1
     zero = jnp.zeros((16, 128), F32)
     for ref, n in ((e, 10), (a_e, 9), (m, 3), (a_m, 3)):
         for k in range(n):
@@ -161,8 +153,8 @@
         low = low_half(iota((16, 128), 1))
         ra = recv_a[zz]
         rb = recv_b[zz]
-        before = jnp.where(even_y, rb, ra)
-        after = jnp.where(even_y, ra, rb)
+        before = jnp.where(odd_y, rb, ra)
+        after = jnp.where(odd_y, ra, rb)
         both = (
             jnp.where(low, before, pltpu.roll(after, EDGE, 1)),
             jnp.where(low, pltpu.roll(before, 128 - EDGE, 1), after),
@@ -209,8 +201,8 @@
                 put_rows(down, DOWN, base + k, f[0:8], 0)
         for t in range(3):
             rows = slice(8 * t, 8 * t + 8)
-            out_a[z, rows] = jnp.where(even_x, up[t], down[t])
-            out_b[z, rows] = jnp.where(even_x, down[t], up[t])
+            out_a[z, rows] = jnp.where(odd_x, up[t], down[t])
+            out_b[z, rows] = jnp.where(odd_x, down[t], up[t])
         return carry
 
     lax.fori_loop(0, 16, body, 0, unroll=UNROLL)
@@ -261,10 +253,10 @@
 ADDED = ((ahead_first, ahead_last), (behind_first, behind_last), (behind_first, behind_last))
 
 
-def step_kernel(sign, base, par, s, pv, pve, b, be, lam, mu, recv_a, recv_b, v_out, s_out, *rest):
+def step_kernel(sign, base, s, pv, pve, b, be, lam, mu, recv_a, recv_b, v_out, s_out, *rest):
     r_out = rest[0] if len(rest) == 4 else None
     vm_ref, ve_ref, vh_ref = rest[-3:]
-    even_x = par[1] == 0
+    odd_x = lax.axis_index("gx") % 2 == 1
     zero = jnp.zeros((16, 128), F32)
     for k in range(3):
         for z in (0, 1, 18, 19):
@@ -273,8 +265,8 @@
     def speeds(z, carry):
         xa = recv_a[z]
         xb = recv_b[z]
-        before = jnp.where(even_x, xb, xa)
-        after = jnp.where(even_x, xa, xb)
+        before = jnp.where(odd_x, xb, xa)
+        after = jnp.where(odd_x, xa, xb)
 
         def halo(item):
             return (get_rows(before, UP, item, 6), get_rows(after, DOWN, item, 0))
@@ -324,9 +316,10 @@
     lax.fori_loop(0, 16, rates, 0, unroll=UNROLL)
 
 
-CHUNK = 4096
+CHUNK = 8192
 TILE = CHUNK // 128
 ROWS = 64
+OWNED = 2048
 
 
 def pieces(x, n):
@@ -379,13 +372,13 @@
 
 
 def sample_kernel(
-    par, cell, chan_raw, weight, recv_a, angle, recv_b, rates, part, part_a, part_b, trig, chan, table, rows, vals
+    cell, chan_raw, weight, recv_a, angle, recv_b, rates, part, part_a, part_b, trig, chan, table, rows, vals
 ):
-    chan[...] = chan_raw[...] - par[2]
-    even_x = par[1] == 0
+    chan[...] = chan_raw[...] - (lax.axis_index("gx") - 1) * OWNED
+    odd_x = lax.axis_index("gx") % 2 == 1
     aa = recv_a[16, 0:16]
     ab = recv_b[16, 0:16]
-    angles = jnp.concatenate([jnp.where(even_x, ab, aa), angle[...], jnp.where(even_x, aa, ab)], axis=0)
+    angles = jnp.concatenate([jnp.where(odd_x, ab, aa), angle[...], jnp.where(odd_x, aa, ab)], axis=0)
     ang = channel_table(angles)
     for k in range(3):
         hi, lo = pieces(rates[k].T, 2)
@@ -426,17 +419,17 @@
     acc = lax.fori_loop(0, 8192 // CHUNK, scatter, jnp.zeros((144, 128), F32))
     total = acc[0:48] + acc[48:96] + acc[96:144]
     part[...] = total[16:32]
-    part_a[...] = jnp.where(even_x, total[32:48], total[0:16])
-    part_b[...] = jnp.where(even_x, total[0:16], total[32:48])
-
-
-def deposit_kernel(par, cell, chan_raw, trig, robust_a, robust, robust_b, pulled, out, chan, vals, acc):
-    chan[...] = chan_raw[...] - par[2]
-    even_x = par[1] == 0
+    part_a[...] = jnp.where(odd_x, total[32:48], total[0:16])
+    part_b[...] = jnp.where(odd_x, total[0:16], total[32:48])
+
+
+def deposit_kernel(cell, chan_raw, trig, robust_a, robust, robust_b, pulled, out, chan, vals, acc):
+    chan[...] = chan_raw[...] - (lax.axis_index("gx") - 1) * OWNED
+    odd_x = lax.axis_index("gx") % 2 == 1
     ra = robust_a[...]
     rb = robust_b[...]
     tab = channel_table(
-        jnp.concatenate([jnp.where(even_x, rb, ra), robust[...], jnp.where(even_x, ra, rb)], axis=0)
+        jnp.concatenate([jnp.where(odd_x, rb, ra), robust[...], jnp.where(odd_x, ra, rb)], axis=0)
     )
 
     def gather(q, carry):
@@ -454,14 +447,15 @@
         c = lanes_of(cell, q)
         hit = iota((128, CHUNK), 0) == c & 127
         b = jnp.concatenate([jnp.where(hit, lanes_of(vals.at[k], q), 0.0).astype(BF16) for k in range(6)], axis=0)
-        acc[...] += dot_nt(one_hot(c >> 7, 256), b)
+        acc[...] += dot_nt(b, one_hot(c >> 7, 256))
         return carry
 
     lax.fori_loop(0, 8192 // CHUNK, place, 0)
     for k in (2, 4, 5):
         out[k] = pulled[k]
     for n, k in enumerate((0, 1, 3)):
-        out[k] = pulled[k] + acc[:, 256 * n : 256 * n + 128] + acc[:, 256 * n + 128 : 256 * n + 256]
+        both = acc[256 * n : 256 * n + 128] + acc[256 * n + 128 : 256 * n + 256]
+        out[k] = pulled[k] + both.T
 
 
 def pairs(axis, first):
@@ -473,14 +467,14 @@
 
 
 def swap(a, b, axis):
-    return (lax.ppermute(a, axis, pairs(axis, 0)), lax.ppermute(b, axis, pairs(axis, 1)))
+    return (lax.ppermute(a, axis, pairs(axis, 1)), lax.ppermute(b, axis, pairs(axis, 0)))
 
 
 def call(kernel, outs, n_in, scratch, name, space=pltpu.VMEM, limit=VMEM_LIMIT):
     return pl.pallas_call(
         kernel,
         out_shape=outs,
-        in_specs=[pl.BlockSpec(memory_space=pltpu.SMEM)] + [pl.BlockSpec(memory_space=space)] * n_in,
+        in_specs=[pl.BlockSpec(memory_space=space)] * n_in,
         out_specs=jax.tree.map(lambda _: whole(), outs),
         scratch_shapes=scratch,
         compiler_params=pltpu.CompilerParams(vmem_limit_bytes=limit),
@@ -503,9 +497,6 @@
     observed,
 ):
     owned = observed.shape[1]
-    gx = lax.axis_index("gx")
-    gy = lax.axis_index("gy")
-    par = jnp.stack([gy % 2, gx % 2, (gx - 1) * owned]).astype(jnp.int32)
     slots = (ROWS, 128)
     cell = gauge_cell.reshape(slots)
     chan = gauge_channel.reshape(slots)
@@ -523,7 +514,7 @@
         pltpu.HBM,
         60 * 1024 * 1024,
     )(
-        par, stress, velocity, adj_stress, adj_velocity, buoyancy
+        stress, velocity, adj_stress, adj_velocity, buoyancy
     )
     ya, yb = swap(msg_a, msg_b, "gy")
 
@@ -537,7 +528,7 @@
         8,
         [m_scratch, m_scratch],
         "pack_x",
-    )(par, stress, velocity, adj_stress, adj_velocity, buoyancy, angle, ya, yb)
+    )(stress, velocity, adj_stress, adj_velocity, buoyancy, angle, ya, yb)
     xa, xb = swap(xa, xb, "gx")
     frame_v, adj_frame_v = pl.pallas_call(
         frame_kernel,
@@ -552,7 +543,7 @@
     buoyancy_edge = edge[9:10]
     velocity_next, stress_next, rates = call(
         functools.partial(step_kernel, 1.0, 0), (speed, tensor, speed), 9, v_scratch, "step"
-    )(par, stress, part_v, frame_v, buoyancy, buoyancy_edge, lame_lambda, shear_modulus, xa, xb)
+    )(stress, part_v, frame_v, buoyancy, buoyancy_edge, lame_lambda, shear_modulus, xa, xb)
 
     tile = shape((16, 128))
     part, part_a, part_b, trig = call(
@@ -566,12 +557,12 @@
             pltpu.VMEM((3,) + slots, F32),
         ],
         "sample",
-    )(par, cell, chan, weight, xa, angle, xb, rates.reshape(3, 256, 128))
+    )(cell, chan, weight, xa, angle, xb, rates.reshape(3, 256, 128))
 
     part_a, part_b = swap(part_a, part_b, "gx")
     adj_velocity_next, pulled = call(
         functools.partial(step_kernel, -1.0, 8), (speed, tensor), 9, v_scratch, "step_adj"
-    )(par, adj_stress, adj_part_v, adj_frame_v, buoyancy, buoyancy_edge, lame_lambda, shear_modulus, xa, xb)
+    )(adj_stress, adj_part_v, adj_frame_v, buoyancy, buoyancy_edge, lame_lambda, shear_modulus, xa, xb)
 
     predicted = part + part_a + part_b
     misfit = predicted - observed.reshape(16, 128)
@@ -585,10 +576,10 @@
         [
             pltpu.VMEM(slots, jnp.int32),
             pltpu.VMEM((7,) + slots, F32),
-            pltpu.VMEM((256, 768), F32),
+            pltpu.VMEM((768, 256), F32),
         ],
         "deposit",
-    )(par, cell, chan, trig, robust_a, robust, robust_b, pulled.reshape(6, 256, 128)).reshape(tensor.shape)
+    )(cell, chan, trig, robust_a, robust, robust_b, pulled.reshape(6, 256, 128)).reshape(tensor.shape)
     return (velocity_next, stress_next, predicted.reshape(1, owned), adj_velocity_next, adj_stress_next)
 
 

time: 75.9 us -> 65.5 us (0.86)
  the two profiles are of different devices: /device:TPU:38 before, /device:TPU:31 now
where the time goes in v2:
time: 65.5 us; the launch traced here: 65.1 us
  starting transfers between devices  39.3 us (60%)
  Pallas kernels  20.7 us (32%)
  waiting for transfers between devices  2.89 us (4%)
  between operations  0.86 us (1%)
  local copies, waits for them, and re-layouts  0.76 us (1%)
    ppermute x4, starting transfers between devices, swap(): lax.ppermute(b, axis, pairs(axis, 0))  22.3 us
    ppermute x4, starting transfers between devices, swap(): lax.ppermute(a, axis, pairs(axis, 1))  17 us
    pallas_call x1, Pallas kernels, shards(): call(sample_kernel, (tile, tile, tile, shape((3,) + slots)), 7, [pltpu.VM...  5.97 us
    pallas_call x1, Pallas kernels, shards(): call(deposit_kernel, shape((6, 256, 128)), 7, [pltpu.VMEM(slots, jnp.int3...  5.54 us
    pallas_call x1, Pallas kernels, shards(): call(pack_y_kernel, (slab, slab), 5, [pltpu.VMEM(f.shape, F32) for f in (...  3.49 us
    ppermute x4, waiting for transfers between devices, swap(): lax.ppermute(b, axis, pairs(axis, 0))  2.88 us
    pallas_call x1, Pallas kernels, shards(): call(pack_x_kernel, (msg, msg, speed, speed, shape((10, 20, 16, 128)), sh...  2.2 us
    pallas_call x1, Pallas kernels, shards(): call(functools.partial(step_kernel, 1.0, 0), (speed, tensor, speed), 9, v...  1.7 us
  transfers between devices with their start and end apart: 8, of which 3 were waited for; matrix products, arithmetic and copies ran while one was open for 0% of the time, Pallas kernels for 3%

profile of v2, /device:TPU:31, one launch (start us, length us, event | category | flops | bytes accessed | tf_op | source)
XLA Modules:
  0.0 65.1 jit_solution(8291023180336420167)
XLA Ops:
  0.6 0.0 copy-start.3
  0.6 0.0 copy-start
  0.7 0.0 copy-start.4
  0.7 0.0 copy-start.1
  0.7 0.0 copy-start.2
  0.7 3.5 %pack_y.1 = (f32[8,16,128]{2,1,0:T(8,128)}, f32[8,16,128]{2,1,0:T(8,128)}) custom-call(f32[6,16,16,128]{3,2,1,0:T(8,128)} %s.8, f32[3,16,16,128]{3,2,1,0:T(8,128)} %v.3, f32[6,16,16,128]{3,2,1,0:T(8,128)} %s.9, f32[3,16,16,128]{3,2,1,0:T(8,128)} %a_v.3, f32[16,16,128]{2,1,0:T(8,128)} %b.7), custom_call_target="tpu_custom_call" | custom-call | tf_op jit(solution)/shard_map/pack_y/pallas_call | solution.py:507
  4.2 3.9 %collective-permute-start = (f32[8,16,128]{2,1,0:T(8,128)}, f32[8,16,128]{2,1,0:T(8,128)S(1)}, u32[]{:S(2)}, u32[]{:S(2)}) collective-permute-start(f32[8,16,128]{2,1,0:T(8,128)} %get-tuple-element.24), channel_id=1, source_target_pairs={{1,2},{2,1},{3,4},{4,3},{5,6},{6,5},{7,8},{8,7},{9,10},{10,9},{11,... | collective-permute-start | bytes 196616 | tf_op jit(solution)/shard_map/ppermute | solution.py:470
  8.1 3.6 %collective-permute-start.1 = (f32[8,16,128]{2,1,0:T(8,128)}, f32[8,16,128]{2,1,0:T(8,128)S(1)}, u32[]{:S(2)}, u32[]{:S(2)}) collective-permute-start(f32[8,16,128]{2,1,0:T(8,128)} %get-tuple-element.25), channel_id=1, source_target_pairs={{0,1},{1,0},{2,3},{3,2},{4,5},{5,4},{6,7},{7,6},{8,9},{9,8},{10,11... | collective-permute-start | bytes 196616 | tf_op jit(solution)/shard_map/ppermute | solution.py:470
  11.7 0.0 collective-permute-done.recv_a
  11.7 1.9 %collective-permute-done.1.recv_b = f32[8,16,128]{2,1,0:T(8,128)S(1)} collective-permute-done((f32[8,16,128]{2,1,0:T(8,128)}, f32[8,16,128]{2,1,0:T(8,128)S(1)}, u32[]{:S(2)}, u32[]{:S(2)}) %collective-permute-start.1) | collective-permute-done | bytes 65568 | tf_op jit(solution)/shard_map/ppermute | solution.py:470
  13.6 0.0 copy-done.3
  13.6 0.0 copy-done
  13.6 0.0 copy-done.4
  13.6 0.0 copy-done.1
  13.7 0.0 copy-done.2
  13.7 0.0 copy-start.9
  13.7 0.7 %copy-done.9 = f32[1,2048]{1,0:T(1,128)S(1)} copy-done((f32[1,2048]{1,0:T(1,128)S(1)}, f32[1,2048]{1,0:T(1,128)}, u32[]{:S(2)}) %copy-start.9) | copy-done | bytes 8216
  14.4 2.2 %pack_x.1 = (f32[17,24,128]{2,1,0:T(8,128)S(1)}, f32[17,24,128]{2,1,0:T(8,128)S(1)}, f32[3,16,16,128]{3,2,1,0:T(8,128)S(1)}, f32[3,16,16,128]{3,2,1,0:T(8,128)S(...) custom-call(f32[6,16,16,128]{3,2,1,0:T(8,128)S(1)} %copy-done, f32[3,16,16,128]{3,2,1,0:T(8,128)S(1)} %copy-done.3, ...), custom_call_target="tpu_custom_call" | custom-call | tf_op jit(solution)/shard_map/pack_x/pallas_call | solution.py:525
  16.6 7.5 %collective-permute-start.2 = (f32[17,24,128]{2,1,0:T(8,128)S(1)}, f32[17,24,128]{2,1,0:T(8,128)S(1)}, u32[]{:S(2)}, u32[]{:S(2)}) collective-permute-start(f32[17,24,128]{2,1,0:T(8,128)S(1)} %get-tuple-element.30), channel_id=1, source_target_pairs={{16,32},{32,16},{48,64},{64,48},{80,96},{96,80},{112,128},{128,112... | collective-permute-start | bytes 626696 | tf_op jit(solution)/shard_map/ppermute | solution.py:470
  24.0 5.7 %collective-permute-start.3 = (f32[17,24,128]{2,1,0:T(8,128)S(1)}, f32[17,24,128]{2,1,0:T(8,128)S(1)}, u32[]{:S(2)}, u32[]{:S(2)}) collective-permute-start(f32[17,24,128]{2,1,0:T(8,128)S(1)} %get-tuple-element.31), channel_id=1, source_target_pairs={{0,16},{16,0},{32,48},{48,32},{64,80},{80,64},{96,112},{112,96},{1... | collective-permute-start | bytes 626696 | tf_op jit(solution)/shard_map/ppermute | solution.py:470
  29.8 0.0 copy-start.5
  29.8 0.0 copy-start.6
  29.8 0.8 %frame.1 = (f32[3,16,16,128]{3,2,1,0:T(8,128)S(1)}, f32[3,16,16,128]{3,2,1,0:T(8,128)S(1)}) custom-call(f32[6,16,16,128]{3,2,1,0:T(8,128)S(1)} %copy-done, f32[6,16,16,128]{3,2,1,0:T(8,128)S(1)} %copy-done.1, f32[10,20,16,128]{3,2,1,0:T(8,128)S(1)} %get-tuple-element.27.e, f32[9,20,16,128]{3,2,1,0:T(8,128)S(1)} %get-tuple-element.28.a_e), custom_call_target="tpu_custom_call" | custom-call | tf_op jit(solution)/shard_map/frame/pallas_call | solution.py:533
  30.6 0.0 copy-start.7
  30.6 0.0 copy-start.8
  30.6 0.0 copy-start.10
  30.6 0.0 collective-permute-done.2.recv_a
  30.6 0.2 collective-permute-done.3.recv_b
  30.8 0.0 copy-done.5
  30.8 0.0 copy-done.6
  30.8 0.0 copy-start.11
  30.8 1.7 %step.1 = (f32[3,16,16,128]{3,2,1,0:T(8,128)}, f32[6,16,16,128]{3,2,1,0:T(8,128)}, f32[3,16,16,128]{3,2,1,0:T(8,128)S(1)}) custom-call(f32[6,16,16,128]{3,2,1,0:T(8,128)S(1)} %copy-done, f32[3,16,16,128]{3,2,1,0:T(8,128)S(1)} %get-tuple-element.26.pv, f32[3,16,16,128]{3,2,1,0:T(8,128)S(1)} %get-tuple-element.29.pve, f32[16,16,128]{2,1,0:T(8,128)S(1)} %copy-done.2, ...), custom_call_target="tpu_custom_call" | custom-call | tf_op jit(solution)/shard_map/step/pallas_call | solution.py:544
  32.5 0.0 copy-done.7
  32.5 0.0 copy-done.8
  32.5 0.0 copy-done.10
  32.5 6.0 %sample.1 = (f32[16,128]{1,0:T(8,128)S(1)}, f32[16,128]{1,0:T(8,128)S(1)}, f32[16,128]{1,0:T(8,128)S(1)}, f32[3,64,128]{2,1,0:T(8,128)S(1)}) custom-call(s32[64,128]{1,0:T(8,128)S(1)} %bitcast.11, s32[64,128]{1,0:T(8,128)S(1)} %bitcast.13, f32[64,128]{1,0:T(8,128)S(1)} %bitcast.17, f32[17,24,128]{2,1,0:T(8,128)S(1)} %collective-permute-done.2.recv_a, ...), custom_call_target="tpu_custom_call" | custom-call | tf_op jit(solution)/shard_map/sample/pallas_call | solution.py:549
  38.5 3.6 %collective-permute-start.4 = (f32[16,128]{1,0:T(8,128)S(1)}, f32[16,128]{1,0:T(8,128)S(1)}, u32[]{:S(2)}, u32[]{:S(2)}) collective-permute-start(f32[16,128]{1,0:T(8,128)S(1)} %get-tuple-element.36), channel_id=1, source_target_pairs={{16,32},{32,16},{48,64},{64,48},{80,96},{96,80},{112,128},{128,112... | collective-permute-start | bytes 24584 | tf_op jit(solution)/shard_map/ppermute | solution.py:470
  42.1 7.7 %collective-permute-start.5 = (f32[16,128]{1,0:T(8,128)S(1)}, f32[16,128]{1,0:T(8,128)S(1)}, u32[]{:S(2)}, u32[]{:S(2)}) collective-permute-start(f32[16,128]{1,0:T(8,128)S(1)} %get-tuple-element.37), channel_id=1, source_target_pairs={{0,16},{16,0},{32,48},{48,32},{64,80},{80,64},{96,112},{112,96},{1... | collective-permute-start | bytes 24584 | tf_op jit(solution)/shard_map/ppermute | solution.py:470
  49.8 0.0 collective-permute-done.4
  49.9 0.8 %collective-permute-done.5 = f32[16,128]{1,0:T(8,128)S(1)} collective-permute-done((f32[16,128]{1,0:T(8,128)S(1)}, f32[16,128]{1,0:T(8,128)S(1)}, u32[]{:S(2)}, u32[]{:S(2)}) %collective-permute-start.5) | collective-permute-done | bytes 8224 | tf_op jit(solution)/shard_map/ppermute | solution.py:470
  50.7 0.0 copy-done.11
  50.7 0.6 rsqrt_multiply_fusion
  51.3 2.0 %collective-permute-start.6 = (f32[16,128]{1,0:T(8,128)S(1)}, f32[16,128]{1,0:T(8,128)S(1)}, u32[]{:S(2)}, u32[]{:S(2)}) collective-permute-start(f32[16,128]{1,0:T(8,128)S(1)} %get-tuple-element.43.robust), channel_id=1, source_target_pairs={{16,32},{32,16},{48,64},{64,48},{80,96},{96,80},{112,128},{128,112... | collective-permute-start | bytes 24584 | tf_op jit(solution)/shard_map/ppermute | solution.py:470
  53.3 5.3 %collective-permute-start.7 = (f32[16,128]{1,0:T(8,128)S(1)}, f32[16,128]{1,0:T(8,128)S(1)}, u32[]{:S(2)}, u32[]{:S(2)}) collective-permute-start(f32[16,128]{1,0:T(8,128)S(1)} %get-tuple-element.43.robust), channel_id=1, source_target_pairs={{0,16},{16,0},{32,48},{48,32},{64,80},{80,64},{96,112},{112,96},{1... | collective-permute-start | bytes 24584 | tf_op jit(solution)/shard_map/ppermute | solution.py:470
  58.6 1.0 %step_adj.1 = (f32[3,16,16,128]{3,2,1,0:T(8,128)}, f32[6,16,16,128]{3,2,1,0:T(8,128)S(1)}) custom-call(f32[6,16,16,128]{3,2,1,0:T(8,128)S(1)} %copy-done.1, f32[3,16,16,128]{3,2,1,0:T(8,128)S(1)} %get-tuple-element.38.pv, f32[3,16,16,128]{3,2,1,0:T(8,128)S(1)} %get-tuple-element.39.pve, f32[16,16,128]{2,1,0:T(8,128)S(1)} %copy-done.2, ...), custom_call_target="tpu_custom_call" | custom-call | tf_op jit(solution)/shard_map/step_adj/pallas_call | solution.py:563
  59.6 0.0 collective-permute-done.6.robust_a
  59.6 0.0 collective-permute-done.7.robust_b
  59.6 5.5 %deposit.1 = f32[6,256,128]{2,1,0:T(8,128)} custom-call(s32[64,128]{1,0:T(8,128)S(1)} %bitcast.12, s32[64,128]{1,0:T(8,128)S(1)} %bitcast.14, f32[3,64,128]{2,1,0:T(8,128)S(1)} %get-tuple-element.41.trig, f32[16,128]{1,0:T(8,128)S(1)} %collective-permute-done.6.robust_a, f32[16,128]{1,0:T(8,128)S(1)} %get-tuple-element.43.robust, ...), custom_call_target="tpu_custom_call" | custom-call | tf_op jit(solution)/shard_map/deposit/pallas_call | solution.py:572
  (1 shorter events, 0.0 us)
Async XLA Ops:
  0.6 13.0 %copy-start.3 = (f32[3,16,16,128]{3,2,1,0:T(8,128)S(1)}, f32[3,16,16,128]{3,2,1,0:T(8,128)}, u32[]{:S(2)}) copy-start(f32[3,16,16,128]{3,2,1,0:T(8,128)} %v.3) | copy-start | bytes 1179652
  0.6 13.0 %copy-start = (f32[6,16,16,128]{3,2,1,0:T(8,128)S(1)}, f32[6,16,16,128]{3,2,1,0:T(8,128)}, u32[]{:S(2)}) copy-start(f32[6,16,16,128]{3,2,1,0:T(8,128)} %s.8) | copy-start | bytes 2359300
  0.7 13.0 %copy-start.4 = (f32[3,16,16,128]{3,2,1,0:T(8,128)S(1)}, f32[3,16,16,128]{3,2,1,0:T(8,128)}, u32[]{:S(2)}) copy-start(f32[3,16,16,128]{3,2,1,0:T(8,128)} %a_v.3) | copy-start | bytes 1179652
  0.7 13.0 %copy-start.1 = (f32[6,16,16,128]{3,2,1,0:T(8,128)S(1)}, f32[6,16,16,128]{3,2,1,0:T(8,128)}, u32[]{:S(2)}) copy-start(f32[6,16,16,128]{3,2,1,0:T(8,128)} %s.9) | copy-start | bytes 2359300
  0.7 13.0 %copy-start.2 = (f32[16,16,128]{2,1,0:T(8,128)S(1)}, f32[16,16,128]{2,1,0:T(8,128)}, u32[]{:S(2)}) copy-start(f32[16,16,128]{2,1,0:T(8,128)} %b.7) | copy-start | bytes 393220
  4.2 7.5 %collective-permute-start = (f32[8,16,128]{2,1,0:T(8,128)}, f32[8,16,128]{2,1,0:T(8,128)S(1)}, u32[]{:S(2)}, u32[]{:S(2)}) collective-permute-start(f32[8,16,128]{2,1,0:T(8,128)} %get-tuple-element.24), channel_id=1, source_target_pairs={{1,2},{2,1},{3,4},{4,3},{5,6},{6,5},{7,8},{8,7},{9,10},{10,9},{11,... | collective-permute-start | bytes 196616 | tf_op jit(solution)/shard_map/ppermute | solution.py:470
  8.1 5.6 %collective-permute-start.1 = (f32[8,16,128]{2,1,0:T(8,128)}, f32[8,16,128]{2,1,0:T(8,128)S(1)}, u32[]{:S(2)}, u32[]{:S(2)}) collective-permute-start(f32[8,16,128]{2,1,0:T(8,128)} %get-tuple-element.25), channel_id=1, source_target_pairs={{0,1},{1,0},{2,3},{3,2},{4,5},{5,4},{6,7},{7,6},{8,9},{9,8},{10,11... | collective-permute-start | bytes 196616 | tf_op jit(solution)/shard_map/ppermute | solution.py:470
  13.7 0.7 %copy-start.9 = (f32[1,2048]{1,0:T(1,128)S(1)}, f32[1,2048]{1,0:T(1,128)}, u32[]{:S(2)}) copy-start(f32[1,2048]{1,0:T(1,128)} %param.22) | copy-start | bytes 24580
  16.6 14.1 %collective-permute-start.2 = (f32[17,24,128]{2,1,0:T(8,128)S(1)}, f32[17,24,128]{2,1,0:T(8,128)S(1)}, u32[]{:S(2)}, u32[]{:S(2)}) collective-permute-start(f32[17,24,128]{2,1,0:T(8,128)S(1)} %get-tuple-element.30), channel_id=1, source_target_pairs={{16,32},{32,16},{48,64},{64,48},{80,96},{96,80},{112,128},{128,112... | collective-permute-start | bytes 626696 | tf_op jit(solution)/shard_map/ppermute | solution.py:470
  24.0 6.8 %collective-permute-start.3 = (f32[17,24,128]{2,1,0:T(8,128)S(1)}, f32[17,24,128]{2,1,0:T(8,128)S(1)}, u32[]{:S(2)}, u32[]{:S(2)}) collective-permute-start(f32[17,24,128]{2,1,0:T(8,128)S(1)} %get-tuple-element.31), channel_id=1, source_target_pairs={{0,16},{16,0},{32,48},{48,32},{64,80},{80,64},{96,112},{112,96},{1... | collective-permute-start | bytes 626696 | tf_op jit(solution)/shard_map/ppermute | solution.py:470
  29.8 1.0 %copy-start.5 = (f32[16,16,128]{2,1,0:T(8,128)S(1)}, f32[16,16,128]{2,1,0:T(8,128)}, u32[]{:S(2)}) copy-start(f32[16,16,128]{2,1,0:T(8,128)} %lam.3) | copy-start | bytes 393220
  29.8 1.0 %copy-start.6 = (f32[16,16,128]{2,1,0:T(8,128)S(1)}, f32[16,16,128]{2,1,0:T(8,128)}, u32[]{:S(2)}) copy-start(f32[16,16,128]{2,1,0:T(8,128)} %mu.3) | copy-start | bytes 393220
  30.6 1.9 %copy-start.7 = (s32[1,1,8192]{2,1,0:T(1,128)S(1)}, s32[1,1,8192]{2,1,0:T(1,128)}, u32[]{:S(2)}) copy-start(s32[1,1,8192]{2,1,0:T(1,128)} %param.19) | copy-start | bytes 98308
  30.6 1.9 %copy-start.8 = (s32[1,1,8192]{2,1,0:T(1,128)S(1)}, s32[1,1,8192]{2,1,0:T(1,128)}, u32[]{:S(2)}) copy-start(s32[1,1,8192]{2,1,0:T(1,128)} %param.20) | copy-start | bytes 98308
  30.6 1.9 %copy-start.10 = (f32[1,1,8192]{2,1,0:T(1,128)S(1)}, f32[1,1,8192]{2,1,0:T(1,128)}, u32[]{:S(2)}) copy-start(f32[1,1,8192]{2,1,0:T(1,128)} %param.21) | copy-start | bytes 98308
  30.8 19.8 %copy-start.11 = (f32[1,2048]{1,0:T(1,128)S(1)}, f32[1,2048]{1,0:T(1,128)}, u32[]{:S(2)}) copy-start(f32[1,2048]{1,0:T(1,128)} %param.23) | copy-start | bytes 24580
  38.5 11.4 %collective-permute-start.4 = (f32[16,128]{1,0:T(8,128)S(1)}, f32[16,128]{1,0:T(8,128)S(1)}, u32[]{:S(2)}, u32[]{:S(2)}) collective-permute-start(f32[16,128]{1,0:T(8,128)S(1)} %get-tuple-element.36), channel_id=1, source_target_pairs={{16,32},{32,16},{48,64},{64,48},{80,96},{96,80},{112,128},{128,112... | collective-permute-start | bytes 24584 | tf_op jit(solution)/shard_map/ppermute | solution.py:470
  42.1 8.5 %collective-permute-start.5 = (f32[16,128]{1,0:T(8,128)S(1)}, f32[16,128]{1,0:T(8,128)S(1)}, u32[]{:S(2)}, u32[]{:S(2)}) collective-permute-start(f32[16,128]{1,0:T(8,128)S(1)} %get-tuple-element.37), channel_id=1, source_target_pairs={{0,16},{16,0},{32,48},{48,32},{64,80},{80,64},{96,112},{112,96},{1... | collective-permute-start | bytes 24584 | tf_op jit(solution)/shard_map/ppermute | solution.py:470
  51.3 8.3 %collective-permute-start.6 = (f32[16,128]{1,0:T(8,128)S(1)}, f32[16,128]{1,0:T(8,128)S(1)}, u32[]{:S(2)}, u32[]{:S(2)}) collective-permute-start(f32[16,128]{1,0:T(8,128)S(1)} %get-tuple-element.43.robust), channel_id=1, source_target_pairs={{16,32},{32,16},{48,64},{64,48},{80,96},{96,80},{112,128},{128,112... | collective-permute-start | bytes 24584 | tf_op jit(solution)/shard_map/ppermute | solution.py:470
  53.3 6.3 %collective-permute-start.7 = (f32[16,128]{1,0:T(8,128)S(1)}, f32[16,128]{1,0:T(8,128)S(1)}, u32[]{:S(2)}, u32[]{:S(2)}) collective-permute-start(f32[16,128]{1,0:T(8,128)S(1)} %get-tuple-element.43.robust), channel_id=1, source_target_pairs={{0,16},{16,0},{32,48},{48,32},{64,80},{80,64},{96,112},{112,96},{1... | collective-permute-start | bytes 24584 | tf_op jit(solution)/shard_map/ppermute | solution.py:470

commit v3 on v2

--- a/solution.py
+++ b/solution.py
@@ -13,6 +13,7 @@
 F32 = jnp.float32
 BF16 = jnp.bfloat16
 VMEM_LIMIT = 40 * 1024 * 1024
+PACK_LIMIT = 53 * 1024 * 1024 + 768 * 1024
 
 N_Y = 19
 EDGE = 3
@@ -140,7 +141,7 @@
     return pltpu.roll(block, turn, 0) if turn else block
 
 
-def pack_x_kernel(s, v, a_s, a_v, b, angle, recv_a, recv_b, out_a, out_b, pv, a_pv, e, a_e, m, a_m):
+def pack_x_kernel(s, v, a_s, a_v, b, recv_a, recv_b, angle, out_a, out_b, pv, a_pv, e, a_e, m, a_m):
     odd_y = lax.axis_index("gy") % 2 == 1
     odd_x = lax.axis_index("gx") % 2 == 1
     zero = jnp.zeros((16, 128), F32)
@@ -381,7 +382,7 @@
     angles = jnp.concatenate([jnp.where(odd_x, ab, aa), angle[...], jnp.where(odd_x, aa, ab)], axis=0)
     ang = channel_table(angles)
     for k in range(3):
-        hi, lo = pieces(rates[k].T, 2)
+        hi, lo = pieces(rates[k].reshape(256, 128).T, 2)
         table[128 * k : 128 * (k + 1)] = hi
         table[384 + 128 * k : 384 + 128 * (k + 1)] = lo
 
@@ -421,6 +422,14 @@
     part[...] = total[16:32]
     part_a[...] = jnp.where(odd_x, total[32:48], total[0:16])
     part_b[...] = jnp.where(odd_x, total[0:16], total[32:48])
+
+
+def forward_kernel(*refs):
+    fields, gauges, outs, scratch = refs[:9], refs[9:13], refs[13:19], refs[19:]
+    speeds, rates, slots = scratch[:3], scratch[3], scratch[4:]
+    step_kernel(1.0, 0, *fields, *outs[:2], rates, *speeds)
+    cell, chan, weight, angle = gauges
+    sample_kernel(cell, chan, weight, fields[7], angle, fields[8], rates, *outs[2:], *slots)
 
 
 def deposit_kernel(cell, chan_raw, trig, robust_a, robust, robust_b, pulled, out, chan, vals, acc):
@@ -512,7 +521,7 @@
         + [pltpu.SemaphoreType.DMA((Y_GROUPS, 5))],
         "pack_y",
         pltpu.HBM,
-        60 * 1024 * 1024,
+        PACK_LIMIT,
     )(
         stress, velocity, adj_stress, adj_velocity, buoyancy
     )
@@ -528,7 +537,7 @@
         8,
         [m_scratch, m_scratch],
         "pack_x",
-    )(stress, velocity, adj_stress, adj_velocity, buoyancy, angle, ya, yb)
+    )(stress, velocity, adj_stress, adj_velocity, buoyancy, ya, yb, angle)
     xa, xb = swap(xa, xb, "gx")
     frame_v, adj_frame_v = pl.pallas_call(
         frame_kernel,
@@ -541,23 +550,24 @@
 
     v_scratch = [pltpu.VMEM((3, 20, 16, 128), F32)] + [pltpu.VMEM((3, 16, 16, 128), F32)] * 2
     buoyancy_edge = edge[9:10]
-    velocity_next, stress_next, rates = call(
-        functools.partial(step_kernel, 1.0, 0), (speed, tensor, speed), 9, v_scratch, "step"
-    )(stress, part_v, frame_v, buoyancy, buoyancy_edge, lame_lambda, shear_modulus, xa, xb)
-
     tile = shape((16, 128))
-    part, part_a, part_b, trig = call(
-        sample_kernel,
-        (tile, tile, tile, shape((3,) + slots)),
-        7,
-        [
+    velocity_next, stress_next, part, part_a, part_b, trig = call(
+        forward_kernel,
+        (speed, tensor, tile, tile, tile, shape((3,) + slots)),
+        13,
+        v_scratch
+        + [
+            pltpu.VMEM((3, 16, 16, 128), F32),
             pltpu.VMEM(slots, jnp.int32),
             pltpu.VMEM((768, 256), BF16),
             pltpu.VMEM((4,) + slots, F32),
             pltpu.VMEM((3,) + slots, F32),
         ],
-        "sample",
-    )(cell, chan, weight, xa, angle, xb, rates.reshape(3, 256, 128))
+        "forward",
+    )(
+        stress, part_v, frame_v, buoyancy, buoyancy_edge, lame_lambda, shear_modulus, xa, xb,
+        cell, chan, weight, angle,
+    )
 
     part_a, part_b = swap(part_a, part_b, "gx")
     adj_velocity_next, pulled = call(

time: 65.5 us -> 64.5 us (0.985)
  Pallas kernels: 20.7 us -> 19.9 us
    pallas_call x2 -> x1, Pallas kernels: 7.67 us -> 7.58 us  [shards(): call(forward_kernel, (speed, tensor, tile, tile, tile, shape((3,) + slots...]
where the time goes in v3:
time: 64.5 us; the launch traced here: 64.1 us
  starting transfers between devices  39.3 us (61%)
  Pallas kernels  19.9 us (31%)
  waiting for transfers between devices  2.61 us (4%)
  between operations  0.9 us (1%)
  local copies, waits for them, and re-layouts  0.77 us (1%)
    ppermute x4, starting transfers between devices, swap(): lax.ppermute(b, axis, pairs(axis, 0))  22.3 us
    ppermute x4, starting transfers between devices, swap(): lax.ppermute(a, axis, pairs(axis, 1))  17.1 us
    pallas_call x1, Pallas kernels, shards(): call(forward_kernel, (speed, tensor, tile, tile, tile, shape((3,) + slots...  7.58 us
    pallas_call x1, Pallas kernels, shards(): call(deposit_kernel, shape((6, 256, 128)), 7, [pltpu.VMEM(slots, jnp.int3...  5.54 us
    pallas_call x1, Pallas kernels, shards(): call(pack_y_kernel, (slab, slab), 5, [pltpu.VMEM(f.shape, F32) for f in (...  2.84 us
    ppermute x4, waiting for transfers between devices, swap(): lax.ppermute(b, axis, pairs(axis, 0))  2.59 us
    pallas_call x1, Pallas kernels, shards(): call(pack_x_kernel, (msg, msg, speed, speed, shape((10, 20, 16, 128)), sh...  2.18 us
  transfers between devices with their start and end apart: 8, of which 3 were waited for; matrix products, arithmetic and copies ran while one was open for 0% of the time, Pallas kernels for 3%

profile of v3, /device:TPU:31, one launch (start us, length us, event | category | flops | bytes accessed | tf_op | source)
XLA Modules:
  0.0 64.1 jit_solution(12275209733820281094)
XLA Ops:
  0.6 0.0 copy-start.3
  0.6 0.0 copy-start.1
  0.7 0.0 copy-start.4
  0.7 0.0 copy-start
  0.7 0.0 copy-start.2
  0.7 2.8 %pack_y.1 = (f32[8,16,128]{2,1,0:T(8,128)S(1)}, f32[8,16,128]{2,1,0:T(8,128)S(1)}) custom-call(f32[6,16,16,128]{3,2,1,0:T(8,128)} %refs_0_.1, f32[3,16,16,128]{3,2,1,0:T(8,128)} %v.3, f32[6,16,16,128]{3,2,1,0:T(8,128)} %s.7, f32[3,16,16,128]{3,2,1,0:T(8,128)} %a_v.3, f32[16,16,128]{2,1,0:T(8,128)} %b.5), custom_call_target="tpu_custom_call" | custom-call | tf_op jit(solution)/shard_map/pack_y/pallas_call | solution.py:516
  3.5 3.9 %collective-permute-start = (f32[8,16,128]{2,1,0:T(8,128)S(1)}, f32[8,16,128]{2,1,0:T(8,128)S(1)}, u32[]{:S(2)}, u32[]{:S(2)}) collective-permute-start(f32[8,16,128]{2,1,0:T(8,128)S(1)} %get-tuple-element.23), channel_id=1, source_target_pairs={{1,2},{2,1},{3,4},{4,3},{5,6},{6,5},{7,8},{8,7},{9,10},{10,9},{11,... | collective-permute-start | bytes 196616 | tf_op jit(solution)/shard_map/ppermute | solution.py:479
  7.4 3.6 %collective-permute-start.1 = (f32[8,16,128]{2,1,0:T(8,128)S(1)}, f32[8,16,128]{2,1,0:T(8,128)S(1)}, u32[]{:S(2)}, u32[]{:S(2)}) collective-permute-start(f32[8,16,128]{2,1,0:T(8,128)S(1)} %get-tuple-element.24), channel_id=1, source_target_pairs={{0,1},{1,0},{2,3},{3,2},{4,5},{5,4},{6,7},{7,6},{8,9},{9,8},{10,11... | collective-permute-start | bytes 196616 | tf_op jit(solution)/shard_map/ppermute | solution.py:479
  11.1 0.0 collective-permute-done.recv_a
  11.1 1.6 %collective-permute-done.1.recv_b = f32[8,16,128]{2,1,0:T(8,128)S(1)} collective-permute-done((f32[8,16,128]{2,1,0:T(8,128)S(1)}, f32[8,16,128]{2,1,0:T(8,128)S(1)}, u32[]{:S(2)}, u32[]{:S(2)}) %collective-permute-start.1) | collective-permute-done | bytes 65568 | tf_op jit(solution)/shard_map/ppermute | solution.py:479
  12.7 0.0 copy-done.3
  12.7 0.0 copy-done.1
  12.7 0.0 copy-done.4
  12.7 0.0 copy-done
  12.7 0.0 copy-done.2
  12.7 0.0 copy-start.10
  12.7 0.7 %copy-done.10 = f32[1,2048]{1,0:T(1,128)S(1)} copy-done((f32[1,2048]{1,0:T(1,128)S(1)}, f32[1,2048]{1,0:T(1,128)}, u32[]{:S(2)}) %copy-start.10) | copy-done | bytes 8216
  13.4 2.2 %pack_x.1 = (f32[17,24,128]{2,1,0:T(8,128)S(1)}, f32[17,24,128]{2,1,0:T(8,128)S(1)}, f32[3,16,16,128]{3,2,1,0:T(8,128)S(1)}, f32[3,16,16,128]{3,2,1,0:T(8,128)S(...) custom-call(f32[6,16,16,128]{3,2,1,0:T(8,128)S(1)} %copy-done.1, f32[3,16,16,128]{3,2,1,0:T(8,128)S(1)} %copy-done.3, ...), custom_call_target="tpu_custom_call" | custom-call | tf_op jit(solution)/shard_map/pack_x/pallas_call | solution.py:534
  15.6 7.5 %collective-permute-start.2 = (f32[17,24,128]{2,1,0:T(8,128)S(1)}, f32[17,24,128]{2,1,0:T(8,128)S(1)}, u32[]{:S(2)}, u32[]{:S(2)}) collective-permute-start(f32[17,24,128]{2,1,0:T(8,128)S(1)} %get-tuple-element.29), channel_id=1, source_target_pairs={{16,32},{32,16},{48,64},{64,48},{80,96},{96,80},{112,128},{128,112... | collective-permute-start | bytes 626696 | tf_op jit(solution)/shard_map/ppermute | solution.py:479
  23.2 5.7 %collective-permute-start.3 = (f32[17,24,128]{2,1,0:T(8,128)S(1)}, f32[17,24,128]{2,1,0:T(8,128)S(1)}, u32[]{:S(2)}, u32[]{:S(2)}) collective-permute-start(f32[17,24,128]{2,1,0:T(8,128)S(1)} %get-tuple-element.30), channel_id=1, source_target_pairs={{0,16},{16,0},{32,48},{48,32},{64,80},{80,64},{96,112},{112,96},{1... | collective-permute-start | bytes 626696 | tf_op jit(solution)/shard_map/ppermute | solution.py:479
  28.9 0.0 copy-start.5
  28.9 0.0 copy-start.6
  28.9 0.0 copy-start.7
  28.9 0.0 copy-start.8
  28.9 0.0 copy-start.9
  28.9 0.0 copy-start.11
  28.9 0.8 %frame.1 = (f32[3,16,16,128]{3,2,1,0:T(8,128)S(1)}, f32[3,16,16,128]{3,2,1,0:T(8,128)S(1)}) custom-call(f32[6,16,16,128]{3,2,1,0:T(8,128)S(1)} %copy-done.1, f32[6,16,16,128]{3,2,1,0:T(8,128)S(1)} %copy-done, f32[10,20,16,128]{3,2,1,0:T(8,128)S(1)} %get-tuple-element.26.e, f32[9,20,16,128]{3,2,1,0:T(8,128)S(1)} %get-tuple-element.27.a_e), custom_call_target="tpu_custom_call" | custom-call | tf_op jit(solution)/shard_map/frame/pallas_call | solution.py:542
  29.7 0.0 copy-start.12
  29.7 0.0 collective-permute-done.2.refs_7_.recv_a
  29.8 0.2 collective-permute-done.3.refs_8_.recv_b
  29.9 0.0 copy-done.5
  29.9 0.0 copy-done.6
  29.9 0.0 copy-done.7
  29.9 0.0 copy-done.8
  29.9 0.0 copy-done.9
  29.9 0.0 copy-done.11
  30.0 7.6 %forward.1 = (f32[3,16,16,128]{3,2,1,0:T(8,128)}, f32[6,16,16,128]{3,2,1,0:T(8,128)}, f32[16,128]{1,0:T(8,128)S(1)}, f32[16,128]{1,0:T(8,128)S(1)}, f32[16,128]{1,0:T(8,128)S(1)}, /*index=5*/f32[3,64,128]{2,1,0:T(8,128)S(1)}) custom-call(f32[6,16,16,128]{3,2,1,0:T(8,128)S(1)} %copy-done.1, f32[3,16,16,128]{3,2,1,0:T(8,128)S(1)} %get-tuple-element.25.refs_1_, ...), custom_call_target="tpu_custom_call" | custom-call | tf_op jit(solution)/shard_map/forward/pallas_call | solution.py:554
  37.5 3.6 %collective-permute-start.4 = (f32[16,128]{1,0:T(8,128)S(1)}, f32[16,128]{1,0:T(8,128)S(1)}, u32[]{:S(2)}, u32[]{:S(2)}) collective-permute-start(f32[16,128]{1,0:T(8,128)S(1)} %get-tuple-element.34), channel_id=1, source_target_pairs={{16,32},{32,16},{48,64},{64,48},{80,96},{96,80},{112,128},{128,112... | collective-permute-start | bytes 24584 | tf_op jit(solution)/shard_map/ppermute | solution.py:479
  41.1 7.7 %collective-permute-start.5 = (f32[16,128]{1,0:T(8,128)S(1)}, f32[16,128]{1,0:T(8,128)S(1)}, u32[]{:S(2)}, u32[]{:S(2)}) collective-permute-start(f32[16,128]{1,0:T(8,128)S(1)} %get-tuple-element.35), channel_id=1, source_target_pairs={{0,16},{16,0},{32,48},{48,32},{64,80},{80,64},{96,112},{112,96},{1... | collective-permute-start | bytes 24584 | tf_op jit(solution)/shard_map/ppermute | solution.py:479
  48.8 0.0 collective-permute-done.4
  48.8 0.8 %collective-permute-done.5 = f32[16,128]{1,0:T(8,128)S(1)} collective-permute-done((f32[16,128]{1,0:T(8,128)S(1)}, f32[16,128]{1,0:T(8,128)S(1)}, u32[]{:S(2)}, u32[]{:S(2)}) %collective-permute-start.5) | collective-permute-done | bytes 8224 | tf_op jit(solution)/shard_map/ppermute | solution.py:479
  49.6 0.6 rsqrt_multiply_fusion
  50.2 2.0 %collective-permute-start.6 = (f32[16,128]{1,0:T(8,128)S(1)}, f32[16,128]{1,0:T(8,128)S(1)}, u32[]{:S(2)}, u32[]{:S(2)}) collective-permute-start(f32[16,128]{1,0:T(8,128)S(1)} %get-tuple-element.41.robust), channel_id=1, source_target_pairs={{16,32},{32,16},{48,64},{64,48},{80,96},{96,80},{112,128},{128,112... | collective-permute-start | bytes 24584 | tf_op jit(solution)/shard_map/ppermute | solution.py:479
  52.3 5.3 %collective-permute-start.7 = (f32[16,128]{1,0:T(8,128)S(1)}, f32[16,128]{1,0:T(8,128)S(1)}, u32[]{:S(2)}, u32[]{:S(2)}) collective-permute-start(f32[16,128]{1,0:T(8,128)S(1)} %get-tuple-element.41.robust), channel_id=1, source_target_pairs={{0,16},{16,0},{32,48},{48,32},{64,80},{80,64},{96,112},{112,96},{1... | collective-permute-start | bytes 24584 | tf_op jit(solution)/shard_map/ppermute | solution.py:479
  57.6 1.0 %step_adj.1 = (f32[3,16,16,128]{3,2,1,0:T(8,128)}, f32[6,16,16,128]{3,2,1,0:T(8,128)S(1)}) custom-call(f32[6,16,16,128]{3,2,1,0:T(8,128)S(1)} %copy-done, f32[3,16,16,128]{3,2,1,0:T(8,128)S(1)} %get-tuple-element.36.pv, f32[3,16,16,128]{3,2,1,0:T(8,128)S(1)} %get-tuple-element.37.pve, f32[16,16,128]{2,1,0:T(8,128)S(1)} %copy-done.2, ...), custom_call_target="tpu_custom_call" | custom-call | tf_op jit(solution)/shard_map/step_adj/pallas_call | solution.py:573
  58.6 0.0 collective-permute-done.6.robust_a
  58.6 0.0 collective-permute-done.7.robust_b
  58.6 5.5 %deposit.1 = f32[6,256,128]{2,1,0:T(8,128)} custom-call(s32[64,128]{1,0:T(8,128)S(1)} %bitcast.10, s32[64,128]{1,0:T(8,128)S(1)} %bitcast.12, f32[3,64,128]{2,1,0:T(8,128)S(1)} %get-tuple-element.39.trig, f32[16,128]{1,0:T(8,128)S(1)} %collective-permute-done.6.robust_a, f32[16,128]{1,0:T(8,128)S(1)} %get-tuple-element.41.robust, ...), custom_call_target="tpu_custom_call" | custom-call | tf_op jit(solution)/shard_map/deposit/pallas_call | solution.py:582
  (2 shorter events, 0.0 us)
Async XLA Ops:
  0.6 12.1 %copy-start.3 = (f32[3,16,16,128]{3,2,1,0:T(8,128)S(1)}, f32[3,16,16,128]{3,2,1,0:T(8,128)}, u32[]{:S(2)}) copy-start(f32[3,16,16,128]{3,2,1,0:T(8,128)} %v.3) | copy-start | bytes 1179652
  0.6 12.1 %copy-start.1 = (f32[6,16,16,128]{3,2,1,0:T(8,128)S(1)}, f32[6,16,16,128]{3,2,1,0:T(8,128)}, u32[]{:S(2)}) copy-start(f32[6,16,16,128]{3,2,1,0:T(8,128)} %refs_0_.1) | copy-start | bytes 2359300
  0.7 12.0 %copy-start.4 = (f32[3,16,16,128]{3,2,1,0:T(8,128)S(1)}, f32[3,16,16,128]{3,2,1,0:T(8,128)}, u32[]{:S(2)}) copy-start(f32[3,16,16,128]{3,2,1,0:T(8,128)} %a_v.3) | copy-start | bytes 1179652
  0.7 12.0 %copy-start = (f32[6,16,16,128]{3,2,1,0:T(8,128)S(1)}, f32[6,16,16,128]{3,2,1,0:T(8,128)}, u32[]{:S(2)}) copy-start(f32[6,16,16,128]{3,2,1,0:T(8,128)} %s.7) | copy-start | bytes 2359300
  0.7 12.0 %copy-start.2 = (f32[16,16,128]{2,1,0:T(8,128)S(1)}, f32[16,16,128]{2,1,0:T(8,128)}, u32[]{:S(2)}) copy-start(f32[16,16,128]{2,1,0:T(8,128)} %b.5) | copy-start | bytes 393220
  3.5 7.5 %collective-permute-start = (f32[8,16,128]{2,1,0:T(8,128)S(1)}, f32[8,16,128]{2,1,0:T(8,128)S(1)}, u32[]{:S(2)}, u32[]{:S(2)}) collective-permute-start(f32[8,16,128]{2,1,0:T(8,128)S(1)} %get-tuple-element.23), channel_id=1, source_target_pairs={{1,2},{2,1},{3,4},{4,3},{5,6},{6,5},{7,8},{8,7},{9,10},{10,9},{11,... | collective-permute-start | bytes 196616 | tf_op jit(solution)/shard_map/ppermute | solution.py:479
  7.4 5.3 %collective-permute-start.1 = (f32[8,16,128]{2,1,0:T(8,128)S(1)}, f32[8,16,128]{2,1,0:T(8,128)S(1)}, u32[]{:S(2)}, u32[]{:S(2)}) collective-permute-start(f32[8,16,128]{2,1,0:T(8,128)S(1)} %get-tuple-element.24), channel_id=1, source_target_pairs={{0,1},{1,0},{2,3},{3,2},{4,5},{5,4},{6,7},{7,6},{8,9},{9,8},{10,11... | collective-permute-start | bytes 196616 | tf_op jit(solution)/shard_map/ppermute | solution.py:479
  12.7 0.7 %copy-start.10 = (f32[1,2048]{1,0:T(1,128)S(1)}, f32[1,2048]{1,0:T(1,128)}, u32[]{:S(2)}) copy-start(f32[1,2048]{1,0:T(1,128)} %param.22) | copy-start | bytes 24580
  15.6 14.1 %collective-permute-start.2 = (f32[17,24,128]{2,1,0:T(8,128)S(1)}, f32[17,24,128]{2,1,0:T(8,128)S(1)}, u32[]{:S(2)}, u32[]{:S(2)}) collective-permute-start(f32[17,24,128]{2,1,0:T(8,128)S(1)} %get-tuple-element.29), channel_id=1, source_target_pairs={{16,32},{32,16},{48,64},{64,48},{80,96},{96,80},{112,128},{128,112... | collective-permute-start | bytes 626696 | tf_op jit(solution)/shard_map/ppermute | solution.py:479
  23.2 6.8 %collective-permute-start.3 = (f32[17,24,128]{2,1,0:T(8,128)S(1)}, f32[17,24,128]{2,1,0:T(8,128)S(1)}, u32[]{:S(2)}, u32[]{:S(2)}) collective-permute-start(f32[17,24,128]{2,1,0:T(8,128)S(1)} %get-tuple-element.30), channel_id=1, source_target_pairs={{0,16},{16,0},{32,48},{48,32},{64,80},{80,64},{96,112},{112,96},{1... | collective-permute-start | bytes 626696 | tf_op jit(solution)/shard_map/ppermute | solution.py:479
  28.9 1.0 %copy-start.5 = (f32[16,16,128]{2,1,0:T(8,128)S(1)}, f32[16,16,128]{2,1,0:T(8,128)}, u32[]{:S(2)}) copy-start(f32[16,16,128]{2,1,0:T(8,128)} %lam.1) | copy-start | bytes 393220
  28.9 1.0 %copy-start.6 = (f32[16,16,128]{2,1,0:T(8,128)S(1)}, f32[16,16,128]{2,1,0:T(8,128)}, u32[]{:S(2)}) copy-start(f32[16,16,128]{2,1,0:T(8,128)} %mu.1) | copy-start | bytes 393220
  28.9 1.0 %copy-start.7 = (s32[1,1,8192]{2,1,0:T(1,128)S(1)}, s32[1,1,8192]{2,1,0:T(1,128)}, u32[]{:S(2)}) copy-start(s32[1,1,8192]{2,1,0:T(1,128)} %param.19) | copy-start | bytes 98308
  28.9 1.0 %copy-start.8 = (s32[1,1,8192]{2,1,0:T(1,128)S(1)}, s32[1,1,8192]{2,1,0:T(1,128)}, u32[]{:S(2)}) copy-start(s32[1,1,8192]{2,1,0:T(1,128)} %param.20) | copy-start | bytes 98308
  28.9 1.0 %copy-start.9 = (f32[1,1,8192]{2,1,0:T(1,128)S(1)}, f32[1,1,8192]{2,1,0:T(1,128)}, u32[]{:S(2)}) copy-start(f32[1,1,8192]{2,1,0:T(1,128)} %param.21) | copy-start | bytes 98308
  28.9 1.0 %copy-start.11 = (f32[1,2048]{1,0:T(1,128)S(1)}, f32[1,2048]{1,0:T(1,128)}, u32[]{:S(2)}) copy-start(f32[1,2048]{1,0:T(1,128)} %param.22) | copy-start | bytes 24580
  29.7 19.9 %copy-start.12 = (f32[1,2048]{1,0:T(1,128)S(1)}, f32[1,2048]{1,0:T(1,128)}, u32[]{:S(2)}) copy-start(f32[1,2048]{1,0:T(1,128)} %param.23) | copy-start | bytes 24580
  37.5 11.3 %collective-permute-start.4 = (f32[16,128]{1,0:T(8,128)S(1)}, f32[16,128]{1,0:T(8,128)S(1)}, u32[]{:S(2)}, u32[]{:S(2)}) collective-permute-start(f32[16,128]{1,0:T(8,128)S(1)} %get-tuple-element.34), channel_id=1, source_target_pairs={{16,32},{32,16},{48,64},{64,48},{80,96},{96,80},{112,128},{128,112... | collective-permute-start | bytes 24584 | tf_op jit(solution)/shard_map/ppermute | solution.py:479
  41.1 8.5 %collective-permute-start.5 = (f32[16,128]{1,0:T(8,128)S(1)}, f32[16,128]{1,0:T(8,128)S(1)}, u32[]{:S(2)}, u32[]{:S(2)}) collective-permute-start(f32[16,128]{1,0:T(8,128)S(1)} %get-tuple-element.35), channel_id=1, source_target_pairs={{0,16},{16,0},{32,48},{48,32},{64,80},{80,64},{96,112},{112,96},{1... | collective-permute-start | bytes 24584 | tf_op jit(solution)/shard_map/ppermute | solution.py:479
  50.2 8.3 %collective-permute-start.6 = (f32[16,128]{1,0:T(8,128)S(1)}, f32[16,128]{1,0:T(8,128)S(1)}, u32[]{:S(2)}, u32[]{:S(2)}) collective-permute-start(f32[16,128]{1,0:T(8,128)S(1)} %get-tuple-element.41.robust), channel_id=1, source_target_pairs={{16,32},{32,16},{48,64},{64,48},{80,96},{96,80},{112,128},{128,112... | collective-permute-start | bytes 24584 | tf_op jit(solution)/shard_map/ppermute | solution.py:479
  52.3 6.3 %collective-permute-start.7 = (f32[16,128]{1,0:T(8,128)S(1)}, f32[16,128]{1,0:T(8,128)S(1)}, u32[]{:S(2)}, u32[]{:S(2)}) collective-permute-start(f32[16,128]{1,0:T(8,128)S(1)} %get-tuple-element.41.robust), channel_id=1, source_target_pairs={{0,16},{16,0},{32,48},{48,32},{64,80},{80,64},{96,112},{112,96},{1... | collective-permute-start | bytes 24584 | tf_op jit(solution)/shard_map/ppermute | solution.py:479
